TPU v7x, 256 devices: a whole 4x4x8 slice. The times are simulated.
256 devices in a mesh: seq: 16 (over y_hi, z), chan: 16 (over x, y_lo, core).
Axes of the slice: x: 4, y: 4 (y_hi: 2, y_lo: 2; y = y_hi * 2 + y_lo), z: 8, core: 2. Of those that a mesh axis runs over, the one named last changes fastest.
Arguments:
- query_act: bfloat16 [4096, 4096], P('chan', 'seq'), may hold values from -6 to 6
- key_act: bfloat16 [4096, 4096], P('chan', 'seq'), may hold values from -6 to 6
- value_act: bfloat16 [4096, 4096], P('chan', 'seq'), may hold values from -6 to 6
- filter_taps: float32 [4096, 4096], P('chan', 'seq'), may hold values from -0.09375 to 0.09375
- skip_gain: float32 [4096], P('chan'), may hold values from -4 to 4
- out_weight: bfloat16 [4096, 8192], P('chan'), may hold values from -0.125 to 0.125
Outputs:
- mixed: bfloat16 [8192, 4096], P('chan', 'seq')
All inputs are finite; a program needn't handle non-finite values.
Results may differ from a plain program's by a relative error of at most 0.025.
Values may be sent and summed in bfloat16 or wider, within the bound.
No kernel may reach another device: no remote copies, remote signals or barrier semaphores. Data moves between devices by JAX's collectives and lax.ppermute only.
A program may use at most 64 MiB of HBM per device.

v0:
```python
import math

import jax
import jax.numpy as jnp
from jax import lax
from jax.sharding import PartitionSpec as P


def from_partner(value, axis, distance):
    mask = 2**distance
    pairs = [(source, source ^ mask) for source in range(lax.axis_size(axis))]
    return lax.ppermute(value, axis, pairs)


def dft_table(length, orient):
    indices = jnp.arange(length, dtype=jnp.int32)
    phase_index = indices[:, None] * indices[None, :] % length
    angles = orient * 2.0 * math.pi / length * phase_index.astype(jnp.float32)
    return (jnp.cos(angles), jnp.sin(angles))


def times_unit(values, cosine, sine_part):
    real_part = values[0] * cosine - values[1] * sine_part
    imag_part = values[0] * sine_part + values[1] * cosine
    return jnp.stack([real_part, imag_part])


def complex_product(left_side, right_side):
    return times_unit(left_side, right_side[0], right_side[1])


def apply_table(values, table_pair, pattern):
    cosine, sine_part = table_pair

    def contract(left_side, right_side):
        return jnp.einsum(pattern, left_side, right_side, precision=lax.Precision.HIGHEST)

    real_part = contract(values[0], cosine) - contract(values[1], sine_part)
    imag_part = contract(values[0], sine_part) + contract(values[1], cosine)
    return jnp.stack([real_part, imag_part])


def build_signals(sequences, shift_cos, shift_sin):
    real_rows = jnp.stack([sequences, sequences * shift_cos])
    imag_rows = jnp.stack([jnp.zeros_like(sequences), -sequences * shift_sin])
    return jnp.stack([real_rows, imag_rows])


def local(query_act, key_act, value_act, filter_taps, skip_gain, out_weight):
    channels, tok_count = key_act.shape
    seq_count = lax.axis_size("seq")
    seq_index = lax.axis_index("seq")
    bit_count = seq_count.bit_length() - 1
    seq_len = seq_count * tok_count
    gated_input = key_act.astype(jnp.float32) * value_act.astype(jnp.float32)
    local_pos = jnp.arange(tok_count, dtype=jnp.int32)
    positions = seq_index * tok_count + local_pos
    shift_angle = math.pi / seq_len * positions.astype(jnp.float32)
    shift_cos = jnp.cos(shift_angle)
    shift_sin = jnp.sin(shift_angle)
    signals = build_signals(jnp.stack([gated_input, filter_taps]), shift_cos, shift_sin)
    current = signals
    for bit_level in range(bit_count - 1, -1, -1):
        half_span = 1 << bit_level
        partner = from_partner(current.astype(jnp.bfloat16), "seq", bit_level).astype(current.dtype)
        is_upper = seq_index // half_span % 2
        rot_angle = -math.pi / half_span * (seq_index % half_span).astype(jnp.float32)
        rotated = times_unit(partner - current, jnp.cos(rot_angle), jnp.sin(rot_angle))
        current = jnp.where(is_upper == 1, rotated, current + partner)
    freq_index = jnp.zeros((), jnp.int32)
    for bit_level in range(bit_count):
        freq_index = freq_index + seq_index // (1 << bit_level) % 2 * (
            1 << bit_count - 1 - bit_level
        )
    turn_angle = -2.0 * math.pi / seq_len * (local_pos * freq_index % seq_len).astype(jnp.float32)
    turn_cos = jnp.cos(turn_angle)
    turn_sin = jnp.sin(turn_angle)
    tok_table = dft_table(tok_count, -1.0)
    spectra = apply_table(times_unit(current, turn_cos, turn_sin), tok_table, "...b,bk->...k")
    product = complex_product(spectra[:, :, 0], spectra[:, :, 1])
    back_table = dft_table(tok_count, 1.0)
    returned = apply_table(product, back_table, "...k,kb->...b")
    returned = times_unit(returned, turn_cos, -turn_sin)
    current = returned
    for bit_level in range(bit_count):
        half_span = 1 << bit_level
        partner = from_partner(current.astype(jnp.bfloat16), "seq", bit_level).astype(current.dtype)
        is_upper = seq_index // half_span % 2
        rot_angle = math.pi / half_span * (seq_index % half_span).astype(jnp.float32)
        rot_cos = jnp.cos(rot_angle)
        rot_sin = jnp.sin(rot_angle)
        lower_new = current + times_unit(partner, rot_cos, rot_sin)
        upper_new = partner - times_unit(current, rot_cos, rot_sin)
        current = jnp.where(is_upper == 1, upper_new, lower_new)
    conv_out = (current[0, 0] + shift_cos * current[0, 1] - shift_sin * current[1, 1]) / (
        2.0 * seq_len
    )
    gated_rows = (
        query_act.astype(jnp.float32) * (conv_out + skip_gain[:, None] * gated_input)
    ).astype(jnp.bfloat16)
    return lax.psum_scatter(
        lax.dot_general(
            out_weight, gated_rows, (((0,), (0,)), ((), ())), preferred_element_type=jnp.float32
        ).astype(jnp.bfloat16),
        "chan",
        scatter_dimension=0,
        tiled=True,
    )


def solution(mesh):
    placed = (
        P("chan", "seq"),
        P("chan", "seq"),
        P("chan", "seq"),
        P("chan", "seq"),
        P("chan"),
        P("chan", None),
    )
    return jax.shard_map(
        local, mesh=mesh, in_specs=placed, out_specs=P("chan", "seq"), check_vma=False
    )
```

profile of v0, /device:TPU:6, one launch (start us, length us, event | category | flops | bytes accessed | tf_op | source)
XLA Modules:
  0.0 349.3 jit_solution(6446797202669720885)
XLA Ops:
  6.6 1.0 fusion.44
  7.6 1.0 fusion.19
  8.7 0.1 pad_bitcast_fusion
  8.8 0.1 maximum_bitcast_fusion
  8.9 1.3 fusion.7
  10.2 3.2 collective-permute-start
  13.6 23.2 %collective-permute-done = bf16[2,2,2,256,256]{4,3,2,1,0:T(8,128)(2,1)S(1)} collective-permute-done((bf16[2,2,2,256,256]{4,3,2,1,0:T(8,128)(2,1)}, bf16[2,2,2,256,256]{4,3,2,1,0:T(8,128)(2,1)S(1)}, u32[]{:S(2)}, u32[]{:S(2)}) %collective-permute-start) | collective-permute-done | bytes 1048608 | tf_op jit(solution)/shard_map/ppermute | solution.py:12
  36.8 0.2 convert_subtract_fusion.3
  37.1 0.7 copy-done.3
  37.8 0.2 multiply_subtract_fusion.4
  38.0 2.9 fusion.117
  40.9 7.2 %collective-permute-start.1 = (bf16[2,2,2,256,256]{4,3,2,1,0:T(8,128)(2,1)}, bf16[2,2,2,256,256]{4,3,2,1,0:T(8,128)(2,1)S(1)}, u32[]{:S(2)}, u32[]{:S(2)}) collective-permute-start(bf16[2,2,2,256,256]{4,3,2,1,0:T(8,128)(2,1)} %get-tuple-element.18), channel_id=1, source_target_pairs={{0,64},{16,80},{32,96},{48,112},{64,0},{80,16},{96,32},{112,48},{1... | collective-permute-start | bytes 3145736 | tf_op jit(solution)/shard_map/ppermute | solution.py:12
  48.3 43.7 %collective-permute-done.1 = bf16[2,2,2,256,256]{4,3,2,1,0:T(8,128)(2,1)S(1)} collective-permute-done((bf16[2,2,2,256,256]{4,3,2,1,0:T(8,128)(2,1)}, bf16[2,2,2,256,256]{4,3,2,1,0:T(8,128)(2,1)S(1)}, u32[]{:S(2)}, u32[]{:S(2)}) %collective-permute-start.1) | collective-permute-done | bytes 1048608 | tf_op jit(solution)/shard_map/ppermute | solution.py:12
  92.0 0.2 convert_subtract_fusion.2
  92.2 0.7 copy-done.4
  93.0 0.2 multiply_subtract_fusion.3
  93.2 3.2 fusion.115
  96.5 3.1 collective-permute-start.2
  99.7 45.0 %collective-permute-done.2 = bf16[2,2,2,256,256]{4,3,2,1,0:T(8,128)(2,1)S(1)} collective-permute-done((bf16[2,2,2,256,256]{4,3,2,1,0:T(8,128)(2,1)}, bf16[2,2,2,256,256]{4,3,2,1,0:T(8,128)(2,1)S(1)}, u32[]{:S(2)}, u32[]{:S(2)}) %collective-permute-start.2) | collective-permute-done | bytes 1048608 | tf_op jit(solution)/shard_map/ppermute | solution.py:12
  144.7 0.2 convert_subtract_fusion.1
  144.9 0.2 multiply_subtract_fusion.2
  145.2 2.1 fusion.113
  147.4 24.7 %collective-permute-done.3 = bf16[2,2,2,256,256]{4,3,2,1,0:T(8,128)(2,1)S(1)} collective-permute-done((bf16[2,2,2,256,256]{4,3,2,1,0:T(8,128)(2,1)}, bf16[2,2,2,256,256]{4,3,2,1,0:T(8,128)(2,1)S(1)}, u32[]{:S(2)}, u32[]{:S(2)}) %collective-permute-start.3) | collective-permute-done | bytes 1048608 | tf_op jit(solution)/shard_map/ppermute | solution.py:12
  172.1 1.8 convert_subtract_fusion
  174.0 0.2 multiply_subtract_fusion.1
  174.1 1.4 copy-done.1
  175.5 0.4 fusion.4
  176.0 2.0 fusion.35
  177.9 2.0 fusion.37
  179.9 2.0 fusion.6
  182.0 2.0 fusion.5
  183.9 0.1 multiply_add_fusion.13
  184.1 1.6 fusion.15
  185.7 1.8 fusion.17
  187.4 1.6 convolution_add_fusion.1
  189.0 1.7 subtract_bitcast_fusion
  190.7 0.4 collective-permute-start.4
  191.1 0.1 add_bitcast_fusion
  191.2 12.1 %collective-permute-done.4 = bf16[2,2,256,256]{3,2,1,0:T(8,128)(2,1)S(1)} collective-permute-done((bf16[2,2,256,256]{3,2,1,0:T(8,128)(2,1)S(1)}, bf16[2,2,256,256]{3,2,1,0:T(8,128)(2,1)S(1)}, u32[]{:S(2)}, u32[]{:S(2)}) %collective-permute-start.4) | collective-permute-done | bytes 524320 | tf_op jit(solution)/shard_map/ppermute | solution.py:12
  203.3 0.1 convert_element_type.150
  203.4 0.1 multiply_subtract_fusion.11
  203.5 0.3 fusion.111
  203.8 0.1 collective-permute-start.5
  204.0 0.1 multiply_subtract_fusion.10
  204.2 23.4 %collective-permute-done.5 = bf16[2,2,256,256]{3,2,1,0:T(8,128)(2,1)S(1)} collective-permute-done((bf16[2,2,256,256]{3,2,1,0:T(8,128)(2,1)S(1)}, bf16[2,2,256,256]{3,2,1,0:T(8,128)(2,1)S(1)}, u32[]{:S(2)}, u32[]{:S(2)}) %collective-permute-start.5) | collective-permute-done | bytes 524320 | tf_op jit(solution)/shard_map/ppermute | solution.py:12
  227.6 0.1 convert_element_type.152
  227.7 0.1 multiply_subtract_fusion.9
  227.8 0.3 fusion.109
  228.1 3.2 collective-permute-start.6
  231.5 0.1 multiply_subtract_fusion.8
  231.6 25.0 %collective-permute-done.6 = bf16[2,2,256,256]{3,2,1,0:T(8,128)(2,1)S(1)} collective-permute-done((bf16[2,2,256,256]{3,2,1,0:T(8,128)(2,1)S(1)}, bf16[2,2,256,256]{3,2,1,0:T(8,128)(2,1)S(1)}, u32[]{:S(2)}, u32[]{:S(2)}) %collective-permute-start.6) | collective-permute-done | bytes 524320 | tf_op jit(solution)/shard_map/ppermute | solution.py:12
  256.6 0.1 convert_element_type.154
  256.7 0.1 multiply_subtract_fusion.7
  256.8 0.3 fusion.107
  257.1 3.3 collective-permute-start.7
  260.6 0.1 multiply_subtract_fusion.6
  260.7 11.9 %collective-permute-done.7 = bf16[2,2,256,256]{3,2,1,0:T(8,128)(2,1)S(1)} collective-permute-done((bf16[2,2,256,256]{3,2,1,0:T(8,128)(2,1)S(1)}, bf16[2,2,256,256]{3,2,1,0:T(8,128)(2,1)S(1)}, u32[]{:S(2)}, u32[]{:S(2)}) %collective-permute-start.7) | collective-permute-done | bytes 524320 | tf_op jit(solution)/shard_map/ppermute | solution.py:12
  272.6 0.1 convert_element_type.156
  272.7 0.1 multiply_subtract_fusion.5
  272.9 0.3 fusion.11
  273.1 1.9 copy-done.5
  275.0 3.4 fusion
  278.5 62.2 %reduce-scatter.2.cloned.1.call-done = bf16[512,256]{0,1:T(8,128)(2,1)} async-done(((bf16[8192,256]{0,1:T(8,128)(2,1)}), bf16[512,256]{0,1:T(8,128)(2,1)}) %reduce-scatter.2.cloned.1.call-update) | async-done | bytes 262160 | tf_op jit(solution)/shard_map/reduce_scatter | solution.py:101
  340.7 1.8 copy.7
  (26 shorter events, 0.4 us)
Async XLA Ops:
  6.5 2.2 copy-start.6
  6.5 334.1 %reduce-scatter.2.cloned.1.call-start = ((), (), s32[]{:S(2)}) async-start(), calls=%async_computation.1 | async-start | bytes 4456448 | tf_op jit(solution)/shard_map/reduce_scatter | solution.py:101
  8.9 28.2 %copy-start.2 = (f32[1,2,2,256,256]{4,3,2,1,0:T(8,128)}, f32[1,2,2,256,256]{4,3,2,1,0:T(8,128)S(1)}, u32[]{:S(2)}) copy-start(f32[1,2,2,256,256]{4,3,2,1,0:T(8,128)S(1)} %maximum_bitcast_fusion) | copy-start | bytes 3145732
  10.2 26.6 %collective-permute-start = (bf16[2,2,2,256,256]{4,3,2,1,0:T(8,128)(2,1)}, bf16[2,2,2,256,256]{4,3,2,1,0:T(8,128)(2,1)S(1)}, u32[]{:S(2)}, u32[]{:S(2)}) collective-permute-start(bf16[2,2,2,256,256]{4,3,2,1,0:T(8,128)(2,1)} %fusion.7), channel_id=1, source_target_pairs={{0,128},{16,144},{32,160},{48,176},{64,192},{80,208},{96,224},{112... | collective-permute-start | bytes 3145736 | tf_op jit(solution)/shard_map/ppermute | solution.py:12
  36.8 1.0 copy-start.3
  40.9 51.3 %copy-start = (f32[2,2,2,256,256]{4,3,2,1,0:T(8,128)}, f32[2,2,2,256,256]{4,3,2,1,0:T(8,128)S(1)}, u32[]{:S(2)}) copy-start(f32[2,2,2,256,256]{4,3,2,1,0:T(8,128)S(1)} %get-tuple-element.19) | copy-start | bytes 6291460
  40.9 51.0 %collective-permute-start.1 = (bf16[2,2,2,256,256]{4,3,2,1,0:T(8,128)(2,1)}, bf16[2,2,2,256,256]{4,3,2,1,0:T(8,128)(2,1)S(1)}, u32[]{:S(2)}, u32[]{:S(2)}) collective-permute-start(bf16[2,2,2,256,256]{4,3,2,1,0:T(8,128)(2,1)} %get-tuple-element.18), channel_id=1, source_target_pairs={{0,64},{16,80},{32,96},{48,112},{64,0},{80,16},{96,32},{112,48},{1... | collective-permute-start | bytes 3145736 | tf_op jit(solution)/shard_map/ppermute | solution.py:12
  92.0 1.0 copy-start.4
  96.5 48.2 %collective-permute-start.2 = (bf16[2,2,2,256,256]{4,3,2,1,0:T(8,128)(2,1)}, bf16[2,2,2,256,256]{4,3,2,1,0:T(8,128)(2,1)S(1)}, u32[]{:S(2)}, u32[]{:S(2)}) collective-permute-start(bf16[2,2,2,256,256]{4,3,2,1,0:T(8,128)(2,1)} %get-tuple-element.16), channel_id=1, source_target_pairs={{0,32},{16,48},{32,0},{48,16},{64,96},{80,112},{96,64},{112,80},{1... | collective-permute-start | bytes 3145736 | tf_op jit(solution)/shard_map/ppermute | solution.py:12
  147.2 24.8 %collective-permute-start.3 = (bf16[2,2,2,256,256]{4,3,2,1,0:T(8,128)(2,1)}, bf16[2,2,2,256,256]{4,3,2,1,0:T(8,128)(2,1)S(1)}, u32[]{:S(2)}, u32[]{:S(2)}) collective-permute-start(bf16[2,2,2,256,256]{4,3,2,1,0:T(8,128)(2,1)} %get-tuple-element.14), channel_id=1, source_target_pairs={{0,16},{16,0},{32,48},{48,32},{64,80},{80,64},{96,112},{112,96},{1... | collective-permute-start | bytes 3145736 | tf_op jit(solution)/shard_map/ppermute | solution.py:12
  173.9 1.6 copy-start.1
  190.7 12.6 %collective-permute-start.4 = (bf16[2,2,256,256]{3,2,1,0:T(8,128)(2,1)S(1)}, bf16[2,2,256,256]{3,2,1,0:T(8,128)(2,1)S(1)}, u32[]{:S(2)}, u32[]{:S(2)}) collective-permute-start(bf16[2,2,256,256]{3,2,1,0:T(8,128)(2,1)S(1)} %fusion.12), channel_id=1, source_target_pairs={{0,16},{16,0},{32,48},{48,32},{64,80},{80,64},{96,112},{112,96},{1... | collective-permute-start | bytes 1572872 | tf_op jit(solution)/shard_map/ppermute | solution.py:12
  203.8 23.8 %collective-permute-start.5 = (bf16[2,2,256,256]{3,2,1,0:T(8,128)(2,1)S(1)}, bf16[2,2,256,256]{3,2,1,0:T(8,128)(2,1)S(1)}, u32[]{:S(2)}, u32[]{:S(2)}) collective-permute-start(bf16[2,2,256,256]{3,2,1,0:T(8,128)(2,1)S(1)} %get-tuple-element.9), channel_id=1, source_target_pairs={{0,32},{16,48},{32,0},{48,16},{64,96},{80,112},{96,64},{112,80},{1... | collective-permute-start | bytes 1572872 | tf_op jit(solution)/shard_map/ppermute | solution.py:12
  228.1 28.4 %collective-permute-start.6 = (bf16[2,2,256,256]{3,2,1,0:T(8,128)(2,1)S(1)}, bf16[2,2,256,256]{3,2,1,0:T(8,128)(2,1)S(1)}, u32[]{:S(2)}, u32[]{:S(2)}) collective-permute-start(bf16[2,2,256,256]{3,2,1,0:T(8,128)(2,1)S(1)} %get-tuple-element.7), channel_id=1, source_target_pairs={{0,64},{16,80},{32,96},{48,112},{64,0},{80,16},{96,32},{112,48},{1... | collective-permute-start | bytes 1572872 | tf_op jit(solution)/shard_map/ppermute | solution.py:12
  257.1 15.4 %collective-permute-start.7 = (bf16[2,2,256,256]{3,2,1,0:T(8,128)(2,1)S(1)}, bf16[2,2,256,256]{3,2,1,0:T(8,128)(2,1)S(1)}, u32[]{:S(2)}, u32[]{:S(2)}) collective-permute-start(bf16[2,2,256,256]{3,2,1,0:T(8,128)(2,1)S(1)} %get-tuple-element.5), channel_id=1, source_target_pairs={{0,128},{16,144},{32,160},{48,176},{64,192},{80,208},{96,224},{112... | collective-permute-start | bytes 1572872 | tf_op jit(solution)/shard_map/ppermute | solution.py:12
  272.8 2.2 copy-start.5
  272.8 2.2 copy-start.7
  272.8 2.2 copy-start.8
  272.8 2.2 copy-start.9
  272.8 2.2 copy-start.10
Sparse Core Ops, SparseCore 0:
  278.6 62.0 reduce-scatter.1
where the time goes:
time: 356 us; the launch traced here: 349 us
  waiting for transfers between devices  271 us (76%)
  starting transfers between devices  20.4 us (6%)
  other arithmetic  18.3 us (5%)
  matrix products  17.9 us (5%)
  between operations  14.8 us (4%)
  local copies, waits for them, and re-layouts  6.7 us (2%)
    ppermute x8, waiting for transfers between devices, from_partner(): return lax.ppermute(value, axis, pairs)  209 us
    reduce_scatter x1, waiting for transfers between devices, local(): lax.psum_scatter(lax.dot_general(out_weight, gated_rows, (((0,), (0,)), (...  62.2 us
    ppermute x8, starting transfers between devices, from_partner(): return lax.ppermute(value, axis, pairs)  20.4 us
    dot_general x8, matrix products, contract(): jnp.einsum(pattern, left_side, right_side, precision=lax.Precision.HIGHEST)  14.5 us
    convert_element_type x8, other arithmetic, local(): current.astype(jnp.bfloat16)  10.6 us
  transfers between devices with their start and end apart: 9, of which 9 were waited for; matrix products, arithmetic and copies ran while one was open for 0% of the time, Pallas kernels for 0%

commit v1 on v0

v1 whole, which is shorter than its diff:
```python
import functools

import jax
import jax.numpy as jnp
from jax import lax
from jax.experimental import pallas as pl
from jax.experimental.pallas import tpu as pltpu
from jax.sharding import PartitionSpec as P

N_SEQ, N_X, N_CHAN = 16, 4, 16
LANES = 128
VMEM = pl.BlockSpec(memory_space=pltpu.VMEM)


def chan_perm(dx, dy, dk):
    return [
        ((x * 2 + y) * 2 + k, ((x + dx) % N_X * 2 + (y ^ dy)) * 2 + (k ^ dk))
        for x in range(N_X)
        for y in range(2)
        for k in range(2)
    ]


def ring_y_perm(step, dk):
    pairs = []
    for y in range(4):
        to = (y + step) % 4
        for z in range(8):
            for x in range(N_X):
                for k in range(2):
                    source = (y // 2 * 8 + z) * N_CHAN + (x * 2 + y % 2) * 2 + k
                    target = (to // 2 * 8 + z) * N_CHAN + (x * 2 + to % 2) * 2 + (k ^ dk)
                    pairs.append((source, target))
    return pairs


def pack_kernel(key_ref, value_ref, taps_ref, out_ref):
    for dst in range(N_SEQ):
        rows = slice(16 * dst, 16 * dst + 16)
        for half in range(2):
            cols = slice(LANES * half, LANES * half + LANES)
            gated = key_ref[rows, cols].astype(jnp.float32) * value_ref[rows, cols].astype(jnp.float32)
            out_ref[dst, 0, half] = gated.astype(jnp.bfloat16)
            out_ref[dst, 1, half] = taps_ref[rows, cols].astype(jnp.bfloat16)


def conv_kernel(recv_ref, out_ref, xs, hs, ys, xpad, lhs, rhs):
    for s in range(N_SEQ):
        for half in range(2):
            a = 2 * s + half
            xs[16 * a : 16 * a + 16, :] = recv_ref[s, 0, half].astype(jnp.float32)
            hs[16 * a : 16 * a + 16, :] = recv_ref[s, 1, half].astype(jnp.float32)
    for b in range(2):
        xpad[b, 0:32, :] = jnp.zeros((32, LANES), jnp.float32)
    lane = lax.broadcasted_iota(jnp.int32, (8, LANES), 1)
    row = lax.broadcasted_iota(jnp.int32, (8, LANES), 0)

    def one(c, b):
        xpad[b, 32:64, :] = xs[pl.ds(c, 32, stride=16), :]
        for d in range(32):
            lhs[b, :, LANES * d : LANES * d + LANES] = xpad[b, 32 - d : 64 - d, :].astype(jnp.bfloat16)
        before = [jnp.zeros((8, LANES), jnp.float32)] * 16
        for i in range(32):
            taps = jnp.broadcast_to(hs[pl.ds(16 * i + c, 1), :], (8, LANES))
            turned = [pltpu.roll(taps, 8 * g, 1, stride=1, stride_axis=0) for g in range(16)]
            tiles = [jnp.where(lane >= row + 8 * g, turned[g], before[g]) for g in range(16)]
            for g in range(0, 16, 2):
                pair = jnp.concatenate([tiles[g], tiles[g + 1]], 0).astype(jnp.bfloat16)
                rhs[b, LANES * i + 8 * g : LANES * i + 8 * g + 16, :] = pair
            before = turned
        ys[pl.ds(c, 32, stride=16), :] = jnp.dot(lhs[b], rhs[b], preferred_element_type=jnp.float32)

    def body(p, carry):
        one(2 * p, 0)
        one(2 * p + 1, 1)
        return carry

    lax.fori_loop(0, 8, body, 0)
    for s in range(N_SEQ):
        for half in range(2):
            a = 2 * s + half
            out_ref[s, half] = ys[16 * a : 16 * a + 16, :].astype(jnp.bfloat16)


def rows_kernel(query_ref, key_ref, value_ref, gain_ref, conv_ref, out_ref):
    for src in range(N_SEQ):
        rows = slice(16 * src, 16 * src + 16)
        gain = gain_ref[rows, :]
        for half in range(2):
            cols = slice(LANES * half, LANES * half + LANES)
            gated = key_ref[rows, cols].astype(jnp.float32) * value_ref[rows, cols].astype(jnp.float32)
            total = conv_ref[src, half].astype(jnp.float32) + gain * gated
            out_ref[rows, cols] = (query_ref[rows, cols].astype(jnp.float32) * total).astype(jnp.bfloat16)


def slice_kernel(place_ref, own, core, ring, diag, own_out, core_out, ring_a, ring_b, diag_a, diag_b):
    own_out[0] = own[...]
    core_out[0] = core[...]
    ring_a[0] = ring[:128, :]
    ring_b[0] = ring[128:, :]
    diag_a[0] = diag[:128, :]
    diag_b[0] = diag[128:, :]


def weight_slices(weight, place):
    def column(dy, dk):
        def index(n, place):
            return (0, ((place[0] + n) % N_X * 2 + (place[1] ^ dy)) * 2 + (place[2] ^ dk))

        return pl.BlockSpec((256, 512), index)

    whole = pl.BlockSpec((1, 256, 512), lambda n, place: (n, 0, 0))
    part = pl.BlockSpec((1, 128, 512), lambda n, place: (n, 0, 0))
    return pl.pallas_call(
        slice_kernel,
        grid_spec=pltpu.PrefetchScalarGridSpec(
            num_scalar_prefetch=1,
            grid=(N_X,),
            in_specs=[column(0, 0), column(0, 1), column(1, 0), column(1, 1)],
            out_specs=[whole, whole, part, part, part, part],
        ),
        out_shape=[jax.ShapeDtypeStruct((N_X, 256, 512), jnp.bfloat16)] * 2
        + [jax.ShapeDtypeStruct((N_X, 128, 512), jnp.bfloat16)] * 4,
        cost_estimate=pl.CostEstimate(flops=0, bytes_accessed=8 * 2**20, transcendentals=0),
        compiler_params=pltpu.CompilerParams(vmem_limit_bytes=16 * 2**20),
        name="weight_slices",
    )(place, weight, weight, weight, weight)


def project_kernel(own_w, core_w, ring_a, ring_b, diag_a, diag_b, own_r, core_r, ring_r, diag_r, out_ref):
    def term(weight, rows):
        return lax.dot_general(weight, rows, (((0,), (0,)), ((), ())), preferred_element_type=jnp.float32)

    total = term(own_w[0], own_r[...])
    total += term(core_w[0], core_r[...])
    total += term(ring_a[0], ring_r[:128, :])
    total += term(ring_b[0], ring_r[128:, :])
    total += term(diag_a[0], diag_r[:128, :])
    total += term(diag_b[0], diag_r[128:, :])
    out_ref[...] = total.astype(out_ref.dtype)


def project(n, weights, rows, dtype):
    whole = pl.BlockSpec((1, 256, 512), lambda i: (n, 0, 0))
    part = pl.BlockSpec((1, 128, 512), lambda i: (n, 0, 0))
    full = pl.BlockSpec((256, 256), lambda i: (0, 0))
    return pl.pallas_call(
        project_kernel,
        grid=(1,),
        out_shape=jax.ShapeDtypeStruct((512, 256), dtype),
        in_specs=[whole, whole, part, part, part, part, full, full, full, full],
        out_specs=pl.BlockSpec((512, 256), lambda i: (0, 0)),
        cost_estimate=pl.CostEstimate(flops=2 * 1024 * 512 * 256, bytes_accessed=2 * 2**20, transcendentals=0),
        compiler_params=pltpu.CompilerParams(vmem_limit_bytes=16 * 2**20),
        name="project",
    )(*weights, *rows)


def local(query_act, key_act, value_act, filter_taps, skip_gain, out_weight):
    chan = lax.axis_index("chan")
    send = pl.pallas_call(
        pack_kernel,
        out_shape=jax.ShapeDtypeStruct((N_SEQ, 2, 2, 16, LANES), jnp.bfloat16),
        in_specs=[VMEM] * 3,
        out_specs=VMEM,
        name="pack",
    )(key_act, value_act, filter_taps)
    place = jnp.stack([chan // 4, chan // 2 % 2, chan % 2]).astype(jnp.int32)
    own_w, core_w, ring_a, ring_b, diag_a, diag_b = weight_slices(out_weight, place)
    both = ("seq", "chan")
    core_w = lax.ppermute(core_w, "chan", chan_perm(0, 0, 1))
    ring_a = lax.ppermute(ring_a, both, ring_y_perm(1, 0))
    ring_b = lax.ppermute(ring_b, both, ring_y_perm(-1, 0))
    diag_a = lax.ppermute(diag_a, both, ring_y_perm(1, 1))
    diag_b = lax.ppermute(diag_b, both, ring_y_perm(-1, 1))
    weights = (own_w, core_w, ring_a, ring_b, diag_a, diag_b)

    recv = lax.all_to_all(send, "seq", 0, 0, tiled=True)
    conv = pl.pallas_call(
        conv_kernel,
        out_shape=jax.ShapeDtypeStruct((N_SEQ, 2, 16, LANES), jnp.bfloat16),
        in_specs=[VMEM],
        out_specs=VMEM,
        scratch_shapes=[pltpu.VMEM((512, LANES), jnp.float32)] * 3
        + [
            pltpu.VMEM((2, 64, LANES), jnp.float32),
            pltpu.VMEM((2, 32, 4096), jnp.bfloat16),
            pltpu.VMEM((2, 4096, LANES), jnp.bfloat16),
        ],
        cost_estimate=pl.CostEstimate(flops=2 * 16 * 4096 * 4096, bytes_accessed=2**20, transcendentals=0),
        compiler_params=pltpu.CompilerParams(vmem_limit_bytes=32 * 2**20),
        name="conv",
    )(recv)
    conv = lax.all_to_all(conv, "seq", 0, 0, tiled=True)
    own_r = pl.pallas_call(
        rows_kernel,
        out_shape=jax.ShapeDtypeStruct((256, 256), jnp.bfloat16),
        in_specs=[VMEM] * 5,
        out_specs=VMEM,
        name="rows",
    )(query_act, key_act, value_act, skip_gain[:, None], conv)
    core_r = lax.ppermute(own_r, "chan", chan_perm(0, 0, 1))
    ring_r = lax.ppermute(own_r, "chan", chan_perm(0, 1, 0))
    diag_r = lax.ppermute(ring_r, "chan", chan_perm(0, 0, 1))
    rows = (own_r, core_r, ring_r, diag_r)
    far = lax.ppermute(project(2, weights, rows, jnp.bfloat16), "chan", chan_perm(2, 0, 0))
    up = lax.ppermute(project(1, weights, rows, jnp.bfloat16), "chan", chan_perm(1, 0, 0))
    down = lax.ppermute(project(3, weights, rows, jnp.bfloat16), "chan", chan_perm(-1, 0, 0))
    own = project(0, weights, rows, jnp.float32)
    total = own + far.astype(jnp.float32) + up.astype(jnp.float32) + down.astype(jnp.float32)
    return total.astype(jnp.bfloat16)


def solution(mesh):
    placed = (
        P("chan", "seq"),
        P("chan", "seq"),
        P("chan", "seq"),
        P("chan", "seq"),
        P("chan"),
        P("chan", None),
    )
    return jax.shard_map(
        local, mesh=mesh, in_specs=placed, out_specs=P("chan", "seq"), check_vma=False
    )
```

time: 356 us -> 80.4 us (0.23); the launches traced: 349 us -> 79.6 us
  waiting for transfers between devices: 271 us -> 22.8 us
  Pallas kernels: 0 us -> 22.2 us
  matrix products: 17.9 us -> 0 us
  other arithmetic: 18.3 us -> 0.89 us
  between operations: 14.8 us -> 0.13 us
  starting transfers between devices: 20.4 us -> 29.1 us
    ppermute x8 -> x11, waiting for transfers between devices: 209 us -> 13.4 us  [the longest x1 4.41 us: local(): ring_r = lax.ppermute(own_r, 'chan', chan_perm(0, 1, 0))]
    reduce_scatter x1 -> x0, waiting for transfers between devices: 62.2 us -> none  [local(): lax.psum_scatter(lax.dot_general(out_weight, gated_rows, (((0,), (0,)), (...]
    pallas_call x0 -> x8, Pallas kernels: none -> 22.2 us  [the longest x1 9.03 us: local(): pl.pallas_call(conv_kernel, out_shape=jax.ShapeDtypeStruct((N_SEQ, 2, 16,...]
    all_to_all x0 -> x2, starting transfers between devices: none -> 18.3 us  [the longest x1 11.2 us: local(): recv = lax.all_to_all(send, 'seq', 0, 0, tiled=True)]
    dot_general x9 -> x0, matrix products: 17.9 us -> none  [the longest x8 14.5 us: contract(): jnp.einsum(pattern, left_side, right_side, precision=lax.Precision.HIGHEST)]
    convert_element_type x12 -> x1, other arithmetic: 10.9 us -> 0.82 us  [local(): return total.astype(jnp.bfloat16)]
    ppermute x8 -> x11, starting transfers between devices: 20.4 us -> 10.8 us  [the longest x1 2.97 us: local(): diag_b = lax.ppermute(diag_b, both, ring_y_perm(-1, 1))]
    all_to_all x0 -> x2, waiting for transfers between devices: none -> 9.37 us  [the longest x1 9.37 us: local(): conv = lax.all_to_all(conv, 'seq', 0, 0, tiled=True)]
  transfers between devices with their start and end apart: 9 -> 13, of which waited for: 9 -> 6; matrix products, arithmetic and copies ran while one was open for 0% -> 1% of each run, Pallas kernels for 0% -> 24%
where the time goes in v1:
time: 80.4 us; the launch traced here: 79.6 us
  starting transfers between devices  29.1 us (36%)
  waiting for transfers between devices  22.8 us (28%)
  Pallas kernels  22.2 us (28%)
  local copies, waits for them, and re-layouts  4.55 us (6%)
  other arithmetic  0.89 us (1%)
    all_to_all x1, starting transfers between devices, local(): recv = lax.all_to_all(send, 'seq', 0, 0, tiled=True)  11.2 us
    all_to_all x1, waiting for transfers between devices, local(): conv = lax.all_to_all(conv, 'seq', 0, 0, tiled=True)  9.37 us
    pallas_call x1, Pallas kernels, local(): pl.pallas_call(conv_kernel, out_shape=jax.ShapeDtypeStruct((N_SEQ, 2, 16,...  9.03 us
    all_to_all x1, starting transfers between devices, local(): conv = lax.all_to_all(conv, 'seq', 0, 0, tiled=True)  7.07 us
    pallas_call x4, Pallas kernels, project(): pl.pallas_call(project_kernel, grid=(1,), out_shape=jax.ShapeDtypeStruct(...  6.31 us
    ppermute x1, waiting for transfers between devices, local(): ring_r = lax.ppermute(own_r, 'chan', chan_perm(0, 1, 0))  4.41 us
    unnamed x8, local copies, waits for them, and re-layouts  3.75 us
    pallas_call x1, Pallas kernels, weight_slices(): pl.pallas_call(slice_kernel, grid_spec=pltpu.PrefetchScalarGridSpec(num_s...  3.08 us
  transfers between devices with their start and end apart: 13, of which 6 were waited for; matrix products, arithmetic and copies ran while one was open for 1% of the time, Pallas kernels for 24%

profile of v1, /device:TPU:6, one launch (start us, length us, event | category | flops | bytes accessed | tf_op | source)
XLA Modules:
  0.0 79.6 jit_solution(13461475503223105368)
XLA Ops:
  0.0 1.8 %pack.1 = bf16[16,2,2,16,128]{4,3,2,1,0:T(8,128)(2,1)} custom-call(bf16[256,256]{1,0:T(8,128)(2,1)} %key_ref.3, bf16[256,256]{1,0:T(8,128)(2,1)} %value_ref.3, f32[256,256]{1,0:T(8,128)} %taps_ref.1), custom_call_target="tpu_custom_call" | custom-call | tf_op jit(solution)/shard_map/pack/pallas_call | solution.py:161
  1.8 11.2 %all-to-all-start = ((bf16[16,2,2,16,128]{4,3,2,1,0:T(8,128)(2,1)}), bf16[16,2,2,16,128]{4,3,2,1,0:T(8,128)(2,1)S(1)}, u32[]{:S(2)}, u32[]{:S(2)}) async-start(bf16[16,2,2,16,128]{4,3,2,1,0:T(8,128)(2,1)} %pack.1), calls=%async_computation | async-start | bytes 524288 | tf_op jit(solution)/shard_map/all_to_all | solution.py:178
  13.1 0.1 pad_add_fusion.place_ref
  13.1 0.0 copy-start
  13.1 2.2 %copy-done = bf16[256,8192]{1,0:T(8,128)(2,1)S(1)} copy-done((bf16[256,8192]{1,0:T(8,128)(2,1)S(1)}, bf16[256,8192]{1,0:T(8,128)(2,1)}, u32[]{:S(2)}) %copy-start) | copy-done | bytes 4194328
  15.3 0.0 copy-start.3
  15.3 3.1 %weight_slices.1 = (bf16[4,256,512]{2,1,0:T(8,128)(2,1)S(1)}, bf16[4,256,512]{2,1,0:T(8,128)(2,1)}, bf16[4,128,512]{2,1,0:T(8,128)(2,1)}, bf16[4,128,512]{2,1,0:...) custom-call(s32[3]{0:T(128)S(1)} %pad_add_fusion.place_ref, bf16[256,8192]{1,0:T(8,128)(2,1)S(1)} %copy-done, ...), custom_call_target="tpu_custom_call" | custom-call | bytes 8388608 | tf_op jit(solution)/shard_map/weight_slices/pallas_call | solution.py:114
  18.4 0.0 collective-permute-start
  18.4 0.7 collective-permute-start.1
  19.1 2.7 %collective-permute-start.2 = (bf16[4,128,512]{2,1,0:T(8,128)(2,1)}, bf16[4,128,512]{2,1,0:T(8,128)(2,1)S(1)}, u32[]{:S(2)}, u32[]{:S(2)}) collective-permute-start(bf16[4,128,512]{2,1,0:T(8,128)(2,1)} %get-tuple-element.14), channel_id=1, source_target_pairs={{0,130},{1,131},{4,134},{5,135},{8,138},{9,139},{12,142},{13,143},... | collective-permute-start | bytes 1572872 | tf_op jit(solution)/shard_map/ppermute | solution.py:173
  21.8 0.0 collective-permute-start.3
  21.8 3.0 %collective-permute-start.4 = (bf16[4,128,512]{2,1,0:T(8,128)(2,1)}, bf16[4,128,512]{2,1,0:T(8,128)(2,1)}, u32[]{:S(2)}, u32[]{:S(2)}) collective-permute-start(bf16[4,128,512]{2,1,0:T(8,128)(2,1)} %get-tuple-element.16), channel_id=1, source_target_pairs={{0,131},{1,130},{4,135},{5,134},{8,139},{9,138},{12,143},{13,142},... | collective-permute-start | bytes 1572872 | tf_op jit(solution)/shard_map/ppermute | solution.py:175
  24.8 0.0 all-to-all-done.recv_ref
  24.8 9.0 %conv.1 = bf16[16,2,16,128]{3,2,1,0:T(8,128)(2,1)} custom-call(bf16[16,2,2,16,128]{4,3,2,1,0:T(8,128)(2,1)S(1)} %all-to-all-done.recv_ref), custom_call_target="tpu_custom_call" | custom-call | flops 536870912 | bytes 1048576 | tf_op jit(solution)/shard_map/conv/pallas_call | solution.py:179
  33.8 7.1 %all-to-all-start.1 = ((bf16[16,2,16,128]{3,2,1,0:T(8,128)(2,1)}), bf16[16,2,16,128]{3,2,1,0:T(8,128)(2,1)S(1)}, u32[]{:S(2)}, u32[]{:S(2)}) async-start(bf16[16,2,16,128]{3,2,1,0:T(8,128)(2,1)} %conv.1), calls=%async_computation.1 | async-start | bytes 262144 | tf_op jit(solution)/shard_map/all_to_all | solution.py:194
  40.9 0.0 copy-done.3
  40.9 0.8 %copy.7.gain_ref = f32[256,1]{1,0:T(8,128)} copy(f32[256,1]{0,1:T(1,128)S(1)} %bitcast.4) | data formatting | bytes 2048 | tf_op jit(solution)/shard_map/broadcast_in_dim | solution.py:201
  41.7 9.4 %all-to-all-done.1.conv_ref = bf16[16,2,16,128]{3,2,1,0:T(8,128)(2,1)S(1)} async-done(((bf16[16,2,16,128]{3,2,1,0:T(8,128)(2,1)}), bf16[16,2,16,128]{3,2,1,0:T(8,128)(2,1)S(1)}, u32[]{:S(2)}, u32[]{:S(2)}) %all-to-all-start.1) | async-done | bytes 131104 | tf_op jit(solution)/shard_map/all_to_all | solution.py:194
  51.0 0.0 copy-start.2
  51.1 0.7 copy-done.2
  51.7 1.9 %rows.1.own_r = bf16[256,256]{1,0:T(8,128)(2,1)} custom-call(bf16[256,256]{1,0:T(8,128)(2,1)} %query_ref.1, bf16[256,256]{1,0:T(8,128)(2,1)} %key_ref.3, bf16[256,256]{1,0:T(8,128)(2,1)} %value_ref.3, f32[256,1]{1,0:T(8,128)} %copy.7.gain_ref, bf16[16,2,16,128]{3,2,1,0:T(8,128)(2,1)} %copy-done.2), custom_call_target="tpu_custom_call" | custom-call | tf_op jit(solution)/shard_map/rows/pallas_call | solution.py:195
  53.6 0.0 collective-permute-done.1.ring_a
  53.6 0.8 collective-permute-start.6
  54.4 0.0 collective-permute-done.2.ring_b
  54.4 0.0 collective-permute-start.5
  54.4 4.4 %collective-permute-done.6.ring_r = bf16[256,256]{1,0:T(8,128)(2,1)S(1)} collective-permute-done((bf16[256,256]{1,0:T(8,128)(2,1)}, bf16[256,256]{1,0:T(8,128)(2,1)S(1)}, u32[]{:S(2)}, u32[]{:S(2)}) %collective-permute-start.6) | collective-permute-done | bytes 131104 | tf_op jit(solution)/shard_map/ppermute | solution.py:203
  58.8 0.0 collective-permute-start.7
  58.8 0.0 collective-permute-done.3.diag_a
  58.8 0.0 collective-permute-done.4.diag_b
  58.8 0.0 collective-permute-done.5.core_r
  58.8 1.3 %collective-permute-done.7.diag_r = bf16[256,256]{1,0:T(8,128)(2,1)S(1)} collective-permute-done((bf16[256,256]{1,0:T(8,128)(2,1)S(1)}, bf16[256,256]{1,0:T(8,128)(2,1)S(1)}, u32[]{:S(2)}, u32[]{:S(2)}) %collective-permute-start.7) | collective-permute-done | bytes 131104 | tf_op jit(solution)/shard_map/ppermute | solution.py:204
  60.2 0.0 collective-permute-done.core_w
  60.2 0.0 copy-start.1
  60.2 0.9 %copy-done.1 = bf16[256,256]{1,0:T(8,128)(2,1)S(1)} copy-done((bf16[256,256]{1,0:T(8,128)(2,1)S(1)}, bf16[256,256]{1,0:T(8,128)(2,1)}, u32[]{:S(2)}) %copy-start.1) | copy-done | bytes 131096
  61.1 1.6 %project.5 = bf16[512,256]{1,0:T(8,128)(2,1)S(1)} custom-call(bf16[4,256,512]{2,1,0:T(8,128)(2,1)S(1)} %get-tuple-element.11.own_w, bf16[4,256,512]{2,1,0:T(8,128)(2,1)S(1)} %collective-permute-done.core_w, bf16[4,128,512]{2,1,0:T(8,128)(2,1)S(1)} %collective-permute-done.1.ring_a, bf16[4,128,512]{2,1,0:T(8,128)(2,1)S(1)} %collective-permute-done.2.ring_b, ...), custom_call_target="tpu_custom_call" | custom-call | flops 268435456 | bytes 2097152 | tf_op jit(solution)/shard_map/project/pallas_call | solution.py:147
  62.7 1.5 %collective-permute-start.8 = (bf16[512,256]{1,0:T(8,128)(2,1)S(1)}, bf16[512,256]{1,0:T(8,128)(2,1)S(1)}, u32[]{:S(2)}, u32[]{:S(2)}) collective-permute-start(bf16[512,256]{1,0:T(8,128)(2,1)S(1)} %project.5), channel_id=1, source_target_pairs={{0,8},{1,9},{2,10},{3,11},{4,12},{5,13},{6,14},{7,15},{8,0},{9,1},... | collective-permute-start | bytes 786440 | tf_op jit(solution)/shard_map/ppermute | solution.py:206
  64.2 1.6 %project.6 = bf16[512,256]{1,0:T(8,128)(2,1)S(1)} custom-call(bf16[4,256,512]{2,1,0:T(8,128)(2,1)S(1)} %get-tuple-element.11.own_w, bf16[4,256,512]{2,1,0:T(8,128)(2,1)S(1)} %collective-permute-done.core_w, bf16[4,128,512]{2,1,0:T(8,128)(2,1)S(1)} %collective-permute-done.1.ring_a, bf16[4,128,512]{2,1,0:T(8,128)(2,1)S(1)} %collective-permute-done.2.ring_b, ...), custom_call_target="tpu_custom_call" | custom-call | flops 268435456 | bytes 2097152 | tf_op jit(solution)/shard_map/project/pallas_call | solution.py:147
  65.7 2.2 %collective-permute-start.9 = (bf16[512,256]{1,0:T(8,128)(2,1)S(1)}, bf16[512,256]{1,0:T(8,128)(2,1)S(1)}, u32[]{:S(2)}, u32[]{:S(2)}) collective-permute-start(bf16[512,256]{1,0:T(8,128)(2,1)S(1)} %project.6), channel_id=1, source_target_pairs={{0,4},{1,5},{2,6},{3,7},{4,8},{5,9},{6,10},{7,11},{8,12},{9,13},{1... | collective-permute-start | bytes 786440 | tf_op jit(solution)/shard_map/ppermute | solution.py:207
  67.9 1.6 %project.7 = bf16[512,256]{1,0:T(8,128)(2,1)S(1)} custom-call(bf16[4,256,512]{2,1,0:T(8,128)(2,1)S(1)} %get-tuple-element.11.own_w, bf16[4,256,512]{2,1,0:T(8,128)(2,1)S(1)} %collective-permute-done.core_w, bf16[4,128,512]{2,1,0:T(8,128)(2,1)S(1)} %collective-permute-done.1.ring_a, bf16[4,128,512]{2,1,0:T(8,128)(2,1)S(1)} %collective-permute-done.2.ring_b, ...), custom_call_target="tpu_custom_call" | custom-call | flops 268435456 | bytes 2097152 | tf_op jit(solution)/shard_map/project/pallas_call | solution.py:147
  69.5 0.1 collective-permute-start.10
  69.6 1.6 %project.4 = f32[512,256]{1,0:T(8,128)S(1)} custom-call(bf16[4,256,512]{2,1,0:T(8,128)(2,1)S(1)} %get-tuple-element.11.own_w, bf16[4,256,512]{2,1,0:T(8,128)(2,1)S(1)} %collective-permute-done.core_w, bf16[4,128,512]{2,1,0:T(8,128)(2,1)S(1)} %collective-permute-done.1.ring_a, bf16[4,128,512]{2,1,0:T(8,128)(2,1)S(1)} %collective-permute-done.2.ring_b, ...), custom_call_target="tpu_custom_call" | custom-call | flops 268435456 | bytes 2097152 | tf_op jit(solution)/shard_map/project/pallas_call | solution.py:147
  71.2 2.2 %collective-permute-done.8 = bf16[512,256]{1,0:T(8,128)(2,1)S(1)} collective-permute-done((bf16[512,256]{1,0:T(8,128)(2,1)S(1)}, bf16[512,256]{1,0:T(8,128)(2,1)S(1)}, u32[]{:S(2)}, u32[]{:S(2)}) %collective-permute-start.8) | collective-permute-done | bytes 262176 | tf_op jit(solution)/shard_map/ppermute | solution.py:206
  73.4 2.6 %collective-permute-done.9 = bf16[512,256]{1,0:T(8,128)(2,1)S(1)} collective-permute-done((bf16[512,256]{1,0:T(8,128)(2,1)S(1)}, bf16[512,256]{1,0:T(8,128)(2,1)S(1)}, u32[]{:S(2)}, u32[]{:S(2)}) %collective-permute-start.9) | collective-permute-done | bytes 262176 | tf_op jit(solution)/shard_map/ppermute | solution.py:207
  76.0 2.8 %collective-permute-done.10 = bf16[512,256]{1,0:T(8,128)(2,1)S(1)} collective-permute-done((bf16[512,256]{1,0:T(8,128)(2,1)S(1)}, bf16[512,256]{1,0:T(8,128)(2,1)S(1)}, u32[]{:S(2)}, u32[]{:S(2)}) %collective-permute-start.10) | collective-permute-done | bytes 262176 | tf_op jit(solution)/shard_map/ppermute | solution.py:208
  78.8 0.8 %add_convert_fusion = bf16[512,256]{1,0:T(8,128)(2,1)} fusion(bf16[512,256]{1,0:T(8,128)(2,1)S(1)} %collective-permute-done.10, bf16[512,256]{1,0:T(8,128)(2,1)S(1)} %collective-permute-done.9, f32[512,256]{1,0:T(8,128)S(1)} %project.4, bf16[512,256]{1,0:T(8,128)(2,1)S(1)} %collective-permute-done.8), kind=kLoop, calls=%fused_computation | loop fusion | flops 917504 | bytes 1572864 | tf_op jit(solution)/shard_map/convert_element_type | solution.py:211
Async XLA Ops:
  1.8 22.9 %all-to-all-start = ((bf16[16,2,2,16,128]{4,3,2,1,0:T(8,128)(2,1)}), bf16[16,2,2,16,128]{4,3,2,1,0:T(8,128)(2,1)S(1)}, u32[]{:S(2)}, u32[]{:S(2)}) async-start(bf16[16,2,2,16,128]{4,3,2,1,0:T(8,128)(2,1)} %pack.1), calls=%async_computation | async-start | bytes 524288 | tf_op jit(solution)/shard_map/all_to_all | solution.py:178
  13.1 2.2 %copy-start = (bf16[256,8192]{1,0:T(8,128)(2,1)S(1)}, bf16[256,8192]{1,0:T(8,128)(2,1)}, u32[]{:S(2)}) copy-start(bf16[256,8192]{1,0:T(8,128)(2,1)} %diag.1) | copy-start | bytes 12582916
  15.3 25.5 %copy-start.3 = (f32[256]{0:T(256)S(1)}, f32[256]{0:T(256)}, u32[]{:S(2)}) copy-start(f32[256]{0:T(256)} %param.10) | copy-start | bytes 3076
  18.4 41.8 %collective-permute-start = (bf16[4,256,512]{2,1,0:T(8,128)(2,1)}, bf16[4,256,512]{2,1,0:T(8,128)(2,1)S(1)}, u32[]{:S(2)}, u32[]{:S(2)}) collective-permute-start(bf16[4,256,512]{2,1,0:T(8,128)(2,1)} %get-tuple-element.12), channel_id=1, source_target_pairs={{0,1},{1,0},{2,3},{3,2},{4,5},{5,4},{6,7},{7,6},{8,9},{9,8},{10,11... | collective-permute-start | bytes 3145736 | tf_op jit(solution)/shard_map/ppermute | solution.py:171
  18.4 35.2 %collective-permute-start.1 = (bf16[4,128,512]{2,1,0:T(8,128)(2,1)}, bf16[4,128,512]{2,1,0:T(8,128)(2,1)S(1)}, u32[]{:S(2)}, u32[]{:S(2)}) collective-permute-start(bf16[4,128,512]{2,1,0:T(8,128)(2,1)} %get-tuple-element.13), channel_id=1, source_target_pairs={{0,2},{1,3},{4,6},{5,7},{8,10},{9,11},{12,14},{13,15},{16,18},{17,... | collective-permute-start | bytes 1572872 | tf_op jit(solution)/shard_map/ppermute | solution.py:172
  19.1 35.3 %collective-permute-start.2 = (bf16[4,128,512]{2,1,0:T(8,128)(2,1)}, bf16[4,128,512]{2,1,0:T(8,128)(2,1)S(1)}, u32[]{:S(2)}, u32[]{:S(2)}) collective-permute-start(bf16[4,128,512]{2,1,0:T(8,128)(2,1)} %get-tuple-element.14), channel_id=1, source_target_pairs={{0,130},{1,131},{4,134},{5,135},{8,138},{9,139},{12,142},{13,143},... | collective-permute-start | bytes 1572872 | tf_op jit(solution)/shard_map/ppermute | solution.py:173
  21.8 37.0 %collective-permute-start.3 = (bf16[4,128,512]{2,1,0:T(8,128)(2,1)}, bf16[4,128,512]{2,1,0:T(8,128)(2,1)}, u32[]{:S(2)}, u32[]{:S(2)}) collective-permute-start(bf16[4,128,512]{2,1,0:T(8,128)(2,1)} %get-tuple-element.15), channel_id=1, source_target_pairs={{0,3},{1,2},{4,7},{5,6},{8,11},{9,10},{12,15},{13,14},{16,19},{17,... | collective-permute-start | bytes 1572872 | tf_op jit(solution)/shard_map/ppermute | solution.py:174
  21.8 37.0 %collective-permute-start.4 = (bf16[4,128,512]{2,1,0:T(8,128)(2,1)}, bf16[4,128,512]{2,1,0:T(8,128)(2,1)}, u32[]{:S(2)}, u32[]{:S(2)}) collective-permute-start(bf16[4,128,512]{2,1,0:T(8,128)(2,1)} %get-tuple-element.16), channel_id=1, source_target_pairs={{0,131},{1,130},{4,135},{5,134},{8,139},{9,138},{12,143},{13,142},... | collective-permute-start | bytes 1572872 | tf_op jit(solution)/shard_map/ppermute | solution.py:175
  33.8 17.3 %all-to-all-start.1 = ((bf16[16,2,16,128]{3,2,1,0:T(8,128)(2,1)}), bf16[16,2,16,128]{3,2,1,0:T(8,128)(2,1)S(1)}, u32[]{:S(2)}, u32[]{:S(2)}) async-start(bf16[16,2,16,128]{3,2,1,0:T(8,128)(2,1)} %conv.1), calls=%async_computation.1 | async-start | bytes 262144 | tf_op jit(solution)/shard_map/all_to_all | solution.py:194
  51.0 0.7 copy-start.2
  53.6 5.2 %collective-permute-start.6 = (bf16[256,256]{1,0:T(8,128)(2,1)}, bf16[256,256]{1,0:T(8,128)(2,1)S(1)}, u32[]{:S(2)}, u32[]{:S(2)}) collective-permute-start(bf16[256,256]{1,0:T(8,128)(2,1)} %rows.1.own_r), channel_id=1, source_target_pairs={{0,2},{1,3},{2,0},{3,1},{4,6},{5,7},{6,4},{7,5},{8,10},{9,11},{10,... | collective-permute-start | bytes 393224 | tf_op jit(solution)/shard_map/ppermute | solution.py:203
  54.4 4.4 %collective-permute-start.5 = (bf16[256,256]{1,0:T(8,128)(2,1)}, bf16[256,256]{1,0:T(8,128)(2,1)S(1)}, u32[]{:S(2)}, u32[]{:S(2)}) collective-permute-start(bf16[256,256]{1,0:T(8,128)(2,1)} %rows.1.own_r), channel_id=1, source_target_pairs={{0,1},{1,0},{2,3},{3,2},{4,5},{5,4},{6,7},{7,6},{8,9},{9,8},{10,11... | collective-permute-start | bytes 393224 | tf_op jit(solution)/shard_map/ppermute | solution.py:202
  58.8 1.3 %collective-permute-start.7 = (bf16[256,256]{1,0:T(8,128)(2,1)S(1)}, bf16[256,256]{1,0:T(8,128)(2,1)S(1)}, u32[]{:S(2)}, u32[]{:S(2)}) collective-permute-start(bf16[256,256]{1,0:T(8,128)(2,1)S(1)} %collective-permute-done.6.ring_r), channel_id=1, source_target_pairs={{0,1},{1,0},{2,3},{3,2},{4,5},{5,4},{6,7},{7,6},{8,9},{9,8},{10,11... | collective-permute-start | bytes 393224 | tf_op jit(solution)/shard_map/ppermute | solution.py:204
  60.2 0.9 %copy-start.1 = (bf16[256,256]{1,0:T(8,128)(2,1)S(1)}, bf16[256,256]{1,0:T(8,128)(2,1)}, u32[]{:S(2)}) copy-start(bf16[256,256]{1,0:T(8,128)(2,1)} %rows.1.own_r) | copy-start | bytes 393220
  62.7 10.7 %collective-permute-start.8 = (bf16[512,256]{1,0:T(8,128)(2,1)S(1)}, bf16[512,256]{1,0:T(8,128)(2,1)S(1)}, u32[]{:S(2)}, u32[]{:S(2)}) collective-permute-start(bf16[512,256]{1,0:T(8,128)(2,1)S(1)} %project.5), channel_id=1, source_target_pairs={{0,8},{1,9},{2,10},{3,11},{4,12},{5,13},{6,14},{7,15},{8,0},{9,1},... | collective-permute-start | bytes 786440 | tf_op jit(solution)/shard_map/ppermute | solution.py:206
  65.7 10.3 %collective-permute-start.9 = (bf16[512,256]{1,0:T(8,128)(2,1)S(1)}, bf16[512,256]{1,0:T(8,128)(2,1)S(1)}, u32[]{:S(2)}, u32[]{:S(2)}) collective-permute-start(bf16[512,256]{1,0:T(8,128)(2,1)S(1)} %project.6), channel_id=1, source_target_pairs={{0,4},{1,5},{2,6},{3,7},{4,8},{5,9},{6,10},{7,11},{8,12},{9,13},{1... | collective-permute-start | bytes 786440 | tf_op jit(solution)/shard_map/ppermute | solution.py:207
  69.5 9.3 %collective-permute-start.10 = (bf16[512,256]{1,0:T(8,128)(2,1)S(1)}, bf16[512,256]{1,0:T(8,128)(2,1)S(1)}, u32[]{:S(2)}, u32[]{:S(2)}) collective-permute-start(bf16[512,256]{1,0:T(8,128)(2,1)S(1)} %project.7), channel_id=1, source_target_pairs={{0,12},{1,13},{2,14},{3,15},{4,0},{5,1},{6,2},{7,3},{8,4},{9,5},{1... | collective-permute-start | bytes 786440 | tf_op jit(solution)/shard_map/ppermute | solution.py:208

commit v2 on v1

v2 whole, which is shorter than its diff:
```python
import functools

import jax
import jax.numpy as jnp
from jax import lax
from jax.experimental import pallas as pl
from jax.experimental.pallas import tpu as pltpu
from jax.sharding import PartitionSpec as P

N_SEQ, N_X, N_CHAN = 16, 4, 16
LANES = 128
VMEM = pl.BlockSpec(memory_space=pltpu.VMEM)
SMEM = pl.BlockSpec(memory_space=pltpu.SMEM)
ANY = pl.BlockSpec(memory_space=pl.ANY)


def chan_perm(dx, dy, dk):
    return [
        ((x * 2 + y) * 2 + k, ((x + dx) % N_X * 2 + (y ^ dy)) * 2 + (k ^ dk))
        for x in range(N_X)
        for y in range(2)
        for k in range(2)
    ]


def ring_y_perm(step, dk):
    pairs = []
    for y in range(4):
        to = (y + step) % 4
        for z in range(8):
            for x in range(N_X):
                for k in range(2):
                    source = (y // 2 * 8 + z) * N_CHAN + (x * 2 + y % 2) * 2 + k
                    target = (to // 2 * 8 + z) * N_CHAN + (x * 2 + to % 2) * 2 + (k ^ dk)
                    pairs.append((source, target))
    return pairs


def seq_y_groups():
    return [
        [seq * N_CHAN + (x * 2 + y) * 2 + k for seq in range(N_SEQ) for y in range(2)]
        for x in range(N_X)
        for k in range(2)
    ]


def pack_kernel(query_ref, key_ref, value_ref, taps_ref, out_ref):
    for dst in range(N_SEQ):
        rows = slice(16 * dst, 16 * dst + 16)
        for half in range(2):
            cols = slice(LANES * half, LANES * half + LANES)
            gated = key_ref[rows, cols].astype(jnp.float32) * value_ref[rows, cols].astype(jnp.float32)
            out_ref[dst, 0, half] = gated.astype(jnp.bfloat16)
            out_ref[dst, 1, half] = taps_ref[rows, cols].astype(jnp.bfloat16)
            out_ref[dst, 2, half] = query_ref[rows, cols]


def conv_kernel(recv_ref, gain_ref, out_ref, xs, hs, ys, xpad, done, sems):
    for s in range(N_SEQ):
        for half in range(2):
            rows = slice(32 * s + 16 * half, 32 * s + 16 * half + 16)
            xs[rows, :] = recv_ref[s, 0, half].astype(jnp.float32)
            hs[rows, :] = recv_ref[s, 1, half].astype(jnp.float32)
    for b in range(2):
        xpad[b, 0:32, :] = jnp.zeros((32, LANES), jnp.float32)
    lane = lax.broadcasted_iota(jnp.int32, (8, LANES), 1)
    row = lax.broadcasted_iota(jnp.int32, (8, LANES), 0)
    inside = [lane + row < LANES - 8 * g for g in range(16)]

    def body(p, carry):
        for b in range(2):
            xpad[b, 32:64, :] = xs[pl.ds(2 * p + b, 32, stride=16), :]
        before = [jnp.zeros((8, LANES), jnp.float32)] * 2
        total = jnp.zeros((64, 2 * LANES), jnp.float32)
        for d in range(32):
            shifted = jnp.concatenate([xpad[b, 32 - d : 64 - d, :] for b in range(2)], 0).astype(jnp.bfloat16)
            blocks = []
            for b in range(2):
                taps = jnp.broadcast_to(hs[pl.ds(16 * d + 2 * p + b, 1), :], (8, LANES))
                tiles = [
                    pltpu.roll(jnp.where(inside[g], taps, before[b]), 8 * g, 1, stride=1, stride_axis=0)
                    for g in range(16)
                ]
                before[b] = taps
                blocks.append(jnp.concatenate(tiles, 0).astype(jnp.bfloat16))
            total += jnp.dot(shifted, jnp.concatenate(blocks, 1), preferred_element_type=jnp.float32)
        ys[pl.ds(2 * p, 32, stride=16), :] = total[:32, :LANES]
        ys[pl.ds(2 * p + 1, 32, stride=16), :] = total[32:, LANES:]
        return carry

    lax.fori_loop(0, 8, body, 0, unroll=2)
    for s in range(N_SEQ):
        for half in range(2):
            rows = slice(32 * s + 16 * half, 32 * s + 16 * half + 16)
            total = ys[rows, :] + gain_ref[...] * xs[rows, :]
            done[s, half] = (recv_ref[s, 2, half].astype(jnp.float32) * total).astype(jnp.bfloat16)
    copies = [pltpu.make_async_copy(done, out_ref.at[:, y], sems.at[y]) for y in range(2)]
    for copy in copies:
        copy.start()
    for copy in copies:
        copy.wait()


def slice_kernel(parts, place_ref, *refs):
    outs, sems = refs[-len(parts) - 1 : -1], refs[-1]
    copies = []
    for number, (other, out) in enumerate(zip(parts, outs)):
        for n in range(N_X):
            column = (place_ref[0] // 4 + n) % N_X * 4 + ((place_ref[0] % 4) ^ other)
            source = refs[0].at[:, pl.ds(pl.multiple_of(column * 512, 512), 512)]
            copies.append(pltpu.make_async_copy(source, out.at[n], sems.at[number, n]))
            copies[-1].start()
    for copy in copies:
        copy.wait()


def weight_slices(parts, weight, place, *after):
    return pl.pallas_call(
        functools.partial(slice_kernel, parts),
        in_specs=[SMEM] + [ANY] * (1 + len(after)),
        out_specs=[VMEM] * len(parts),
        out_shape=[jax.ShapeDtypeStruct((N_X, 256, 512), jnp.bfloat16)] * len(parts),
        scratch_shapes=[pltpu.SemaphoreType.DMA((len(parts), N_X))],
        cost_estimate=pl.CostEstimate(flops=0, bytes_accessed=len(parts) * 2**20, transcendentals=0),
        compiler_params=pltpu.CompilerParams(vmem_limit_bytes=8 * 2**20),
        name="weight_slices",
    )(place, weight, *after)


def by_position(rows_ref, y):
    halves = [jnp.concatenate([rows_ref[src, y, half] for src in range(N_SEQ)], 0) for half in range(2)]
    return jnp.concatenate([half.astype(jnp.float32).T.astype(jnp.bfloat16) for half in halves], 0)


def mine_kernel(place_ref, own_w, ring_w, rows_ref, *outs):
    y = place_ref[0] // 2 % 2
    own, ring = by_position(rows_ref, y), by_position(rows_ref, 1 - y)
    for n in range(N_X):
        total = jnp.dot(own, own_w[n], preferred_element_type=jnp.float32)
        outs[n][...] = total + jnp.dot(ring, ring_w[n], preferred_element_type=jnp.float32)


def mine_terms(place, own_w, ring_w, rows):
    return pl.pallas_call(
        mine_kernel,
        out_shape=[jax.ShapeDtypeStruct((256, 512), jnp.float32)] * N_X,
        in_specs=[SMEM] + [VMEM] * 3,
        out_specs=[VMEM] * N_X,
        cost_estimate=pl.CostEstimate(flops=2 * 512 * 2048 * 256, bytes_accessed=2**20, transcendentals=0),
        compiler_params=pltpu.CompilerParams(vmem_limit_bytes=12 * 2**20),
        name="mine_terms",
    )(place, own_w, ring_w, rows)


def far_kernel(place_ref, mine, core_w, diag_w, rows_ref, out_ref, core_ref):
    y = place_ref[0] // 2 % 2
    core_ref[:, :256] = by_position(rows_ref, y)
    core_ref[:, 256:] = by_position(rows_ref, 1 - y)
    core_kernel(2, mine, core_w, diag_w, core_ref, None, out_ref)


def far_term(place, mine, core_w, diag_w, rows):
    return pl.pallas_call(
        far_kernel,
        out_shape=[jax.ShapeDtypeStruct((256, 512), jnp.bfloat16)] * 2,
        in_specs=[SMEM] + [VMEM] * 4,
        out_specs=[VMEM] * 2,
        cost_estimate=pl.CostEstimate(flops=2 * 512 * 512 * 256, bytes_accessed=2**20, transcendentals=0),
        compiler_params=pltpu.CompilerParams(vmem_limit_bytes=8 * 2**20),
        name="far_term",
    )(place, mine, core_w, diag_w, rows)


def core_kernel(n, mine, core_w, diag_w, core_r, after, out_ref):
    total = mine[...] + jnp.dot(core_r[:, :256], core_w[n], preferred_element_type=jnp.float32)
    total += jnp.dot(core_r[:, 256:], diag_w[n], preferred_element_type=jnp.float32)
    out_ref[...] = total.astype(out_ref.dtype)


def add_core(n, mine, core_w, diag_w, core_r, after, dtype):
    return pl.pallas_call(
        functools.partial(core_kernel, n),
        out_shape=jax.ShapeDtypeStruct((256, 512), dtype),
        in_specs=[VMEM] * 4 + [ANY],
        out_specs=VMEM,
        cost_estimate=pl.CostEstimate(flops=2 * 512 * 512 * 256, bytes_accessed=2**20, transcendentals=0),
        compiler_params=pltpu.CompilerParams(vmem_limit_bytes=8 * 2**20),
        name="add_core",
    )(mine, core_w, diag_w, core_r, after)


def two_kernel(own, far, out_ref):
    out_ref[...] = own[...] + far[...].astype(jnp.float32)


def sum_kernel(two, up, down, out_ref):
    total = two[...] + up[...].astype(jnp.float32) + down[...].astype(jnp.float32)
    out_ref[...] = total.T.astype(jnp.bfloat16)


def local(query_act, key_act, value_act, filter_taps, skip_gain, out_weight):
    chan = lax.axis_index("chan")
    both = ("seq", "chan")
    send = pl.pallas_call(
        pack_kernel,
        out_shape=jax.ShapeDtypeStruct((N_SEQ, 3, 2, 16, LANES), jnp.bfloat16),
        in_specs=[VMEM] * 4,
        out_specs=VMEM,
        name="pack",
    )(query_act, key_act, value_act, filter_taps)
    place = jnp.reshape(chan, (1,)).astype(jnp.int32)
    own_w, core_w, ring_w, diag_w = weight_slices((0, 1, 2, 3), out_weight, place, send)
    ring_w = lax.ppermute(ring_w, both, ring_y_perm(1, 0))
    diag_w = lax.ppermute(diag_w, both, ring_y_perm(-1, 1))
    core_w = lax.ppermute(core_w, "chan", chan_perm(0, 0, 1))

    gain = lax.dynamic_slice(skip_gain, (16 * lax.axis_index("seq"),), (16,))
    gain = jnp.broadcast_to(gain[:, None], (16, LANES))
    recv = lax.all_to_all(send, "seq", 0, 0, tiled=True)
    rows = pl.pallas_call(
        conv_kernel,
        out_shape=jax.ShapeDtypeStruct((N_SEQ, 2, 2, 16, LANES), jnp.bfloat16),
        in_specs=[VMEM, VMEM],
        out_specs=ANY,
        scratch_shapes=[pltpu.VMEM((512, LANES), jnp.float32)] * 3
        + [
            pltpu.VMEM((2, 64, LANES), jnp.float32),
            pltpu.VMEM((N_SEQ, 2, 16, LANES), jnp.bfloat16),
            pltpu.SemaphoreType.DMA((2,)),
        ],
        cost_estimate=pl.CostEstimate(flops=2 * 16 * 4096 * 4096, bytes_accessed=0, transcendentals=0),
        compiler_params=pltpu.CompilerParams(vmem_limit_bytes=8 * 2**20),
        name="conv",
    )(recv, gain)
    rows = jnp.reshape(rows, (2 * N_SEQ, 2, 16, LANES))
    rows = lax.all_to_all(rows, both, 0, 0, axis_index_groups=seq_y_groups(), tiled=True)
    rows = jnp.reshape(rows, (N_SEQ, 2, 2, 16, LANES))
    core_rows = lax.ppermute(rows, "chan", chan_perm(0, 0, 1))
    terms = mine_terms(place, own_w, ring_w, rows)
    far, core_r = far_term(place, terms[2], core_w, diag_w, core_rows)
    more = (core_w, diag_w, core_r)
    up = add_core(1, terms[1], *more, far, jnp.bfloat16)
    down = add_core(3, terms[3], *more, up, jnp.bfloat16)
    own = add_core(0, terms[0], *more, down, jnp.float32)
    far = lax.ppermute(far, "chan", chan_perm(2, 0, 0))
    up = lax.ppermute(up, "chan", chan_perm(1, 0, 0))
    down = lax.ppermute(down, "chan", chan_perm(-1, 0, 0))
    two = pl.pallas_call(
        two_kernel,
        out_shape=jax.ShapeDtypeStruct((256, 512), jnp.float32),
        in_specs=[VMEM] * 2,
        out_specs=VMEM,
        compiler_params=pltpu.CompilerParams(vmem_limit_bytes=4 * 2**20),
        name="two",
    )(own, far)
    return pl.pallas_call(
        sum_kernel,
        out_shape=jax.ShapeDtypeStruct((512, 256), jnp.bfloat16),
        in_specs=[VMEM] * 3,
        out_specs=VMEM,
        compiler_params=pltpu.CompilerParams(vmem_limit_bytes=4 * 2**20),
        name="sum",
    )(two, up, down)


def solution(mesh):
    placed = (
        P("chan", "seq"),
        P("chan", "seq"),
        P("chan", "seq"),
        P("chan", "seq"),
        P("chan"),
        P("chan", None),
    )
    return jax.shard_map(
        local, mesh=mesh, in_specs=placed, out_specs=P("chan", "seq"), check_vma=False
    )
```

time: 80.4 us -> 71.6 us (0.89)
  blocking collectives: 0 us -> 18.2 us
  starting transfers between devices: 29.1 us -> 19.6 us
  Pallas kernels: 22.2 us -> 13.8 us
  waiting for transfers between devices: 22.8 us -> 15.2 us
  local copies, waits for them, and re-layouts: 4.55 us -> 3.33 us
  other arithmetic: 0.89 us -> 0 us
    all_to_all x0 -> x1, blocking collectives: none -> 18.2 us  [local(): lax.all_to_all(rows, both, 0, 0, axis_index_groups=seq_y_groups(), tiled=...]
    all_to_all x1 -> x0, waiting for transfers between devices: 9.37 us -> none  [local(): conv = lax.all_to_all(conv, 'seq', 0, 0, tiled=True)]
    pallas_call x8 -> x10, Pallas kernels: 22.2 us -> 13.8 us  [the longest x1 5.36 us: local(): pl.pallas_call(conv_kernel, out_shape=jax.ShapeDtypeStruct((N_SEQ, 2, 2,...]
    all_to_all x1 -> x0, starting transfers between devices: 7.07 us -> none  [local(): conv = lax.all_to_all(conv, 'seq', 0, 0, tiled=True)]
    all_to_all x1, waiting for transfers between devices: 0.01 us -> 5.04 us  [local(): recv = lax.all_to_all(send, 'seq', 0, 0, tiled=True)]
    ppermute x10 -> x6, waiting for transfers between devices: 13.4 us -> 10.2 us  [the longest x1 5.14 us: local(): down = lax.ppermute(down, 'chan', chan_perm(-1, 0, 0))]
    ppermute x10 -> x6, starting transfers between devices: 10.8 us -> 8.35 us  [the longest x1 3.22 us: local(): up = lax.ppermute(up, 'chan', chan_perm(1, 0, 0))]
    convert_element_type x1 -> x0, other arithmetic: 0.82 us -> none  [local(): return total.astype(jnp.bfloat16)]
  transfers between devices with their start and end apart: 13 -> 8, of which waited for: 6 -> 3; matrix products, arithmetic and copies ran while one was open for 1% -> 0% of each run, Pallas kernels for 24% -> 15%
where the time goes in v2:
time: 71.6 us; the launch traced here: 70.3 us
  starting transfers between devices  19.6 us (27%)
  blocking collectives  18.2 us (25%)
  waiting for transfers between devices  15.2 us (21%)
  Pallas kernels  13.8 us (19%)
  local copies, waits for them, and re-layouts  3.33 us (5%)
    all_to_all x1, blocking collectives, local(): lax.all_to_all(rows, both, 0, 0, axis_index_groups=seq_y_groups(), tiled=...  18.2 us
    all_to_all x1, starting transfers between devices, local(): recv = lax.all_to_all(send, 'seq', 0, 0, tiled=True)  11.2 us
    pallas_call x1, Pallas kernels, local(): pl.pallas_call(conv_kernel, out_shape=jax.ShapeDtypeStruct((N_SEQ, 2, 2,...  5.36 us
    ppermute x1, waiting for transfers between devices, local(): down = lax.ppermute(down, 'chan', chan_perm(-1, 0, 0))  5.14 us
    all_to_all x1, waiting for transfers between devices, local(): recv = lax.all_to_all(send, 'seq', 0, 0, tiled=True)  5.04 us
    ppermute x1, waiting for transfers between devices, local(): far = lax.ppermute(far, 'chan', chan_perm(2, 0, 0))  5.01 us
    ppermute x1, starting transfers between devices, local(): up = lax.ppermute(up, 'chan', chan_perm(1, 0, 0))  3.22 us
    unnamed x6, local copies, waits for them, and re-layouts  3.18 us
  transfers between devices with their start and end apart: 8, of which 3 were waited for; matrix products, arithmetic and copies ran while one was open for 0% of the time, Pallas kernels for 15%

profile of v2, /device:TPU:6, one launch (start us, length us, event | category | flops | bytes accessed | tf_op | source)
XLA Modules:
  0.0 70.3 jit_solution(12627245287358875922)
XLA Ops:
  0.0 0.0 copy-start.2
  0.0 2.0 %pack.1.refs_1_ = bf16[16,3,2,16,128]{4,3,2,1,0:T(8,128)(2,1)} custom-call(bf16[256,256]{1,0:T(8,128)(2,1)} %query_ref.1, bf16[256,256]{1,0:T(8,128)(2,1)} %key_ref.1, bf16[256,256]{1,0:T(8,128)(2,1)} %value_ref.1, f32[256,256]{1,0:T(8,128)} %taps_ref.1), custom_call_target="tpu_custom_call" | custom-call | tf_op jit(solution)/shard_map/pack/pallas_call | solution.py:204
  2.0 11.2 %all-to-all-start = ((bf16[16,3,2,16,128]{4,3,2,1,0:T(8,128)(2,1)}), bf16[16,3,2,16,128]{4,3,2,1,0:T(8,128)(2,1)S(1)}, u32[]{:S(2)}, u32[]{:S(2)}) async-start(bf16[16,3,2,16,128]{4,3,2,1,0:T(8,128)(2,1)} %pack.1.refs_1_), calls=%async_computation | async-start | bytes 786432 | tf_op jit(solution)/shard_map/all_to_all | solution.py:219
  13.2 0.0 copy-start
  13.2 2.2 %copy-done = bf16[256,8192]{1,0:T(8,128)(2,1)S(1)} copy-done((bf16[256,8192]{1,0:T(8,128)(2,1)S(1)}, bf16[256,8192]{1,0:T(8,128)(2,1)}, u32[]{:S(2)}) %copy-start) | copy-done | bytes 4194328
  15.4 0.0 copy-start.1
  15.4 1.0 %copy-done.1 = bf16[16,3,2,16,128]{4,3,2,1,0:T(8,128)(2,1)S(1)} copy-done((bf16[16,3,2,16,128]{4,3,2,1,0:T(8,128)(2,1)S(1)}, bf16[16,3,2,16,128]{4,3,2,1,0:T(8,128)(2,1)}, u32[]{:S(2)}) %copy-start.1) | copy-done | bytes 393240
  16.4 2.4 %weight_slices.1 = (bf16[4,256,512]{2,1,0:T(8,128)(2,1)S(1)}, bf16[4,256,512]{2,1,0:T(8,128)(2,1)}, bf16[4,256,512]{2,1,0:T(8,128)(2,1)}, bf16[4,256,512]{2,1,0:T(8,128)(2,1)}) custom-call(s32[1]{0:T(128)} %bitcast.place_ref, bf16[256,8192]{1,0:T(8,128)(2,1)S(1)} %copy-done, bf16[16,3,2,16,128]{4,3,2,1,0:T(8,128)(2,1)S(1)} %copy-done.1), custom_call_target="tpu_custom_call" | custom-call | bytes 4194304 | tf_op jit(solution)/shard_map/weight_slices/pallas_call | solution.py:118
  18.7 0.8 %collective-permute-start = (bf16[4,256,512]{2,1,0:T(8,128)(2,1)}, bf16[4,256,512]{2,1,0:T(8,128)(2,1)}, u32[]{:S(2)}, u32[]{:S(2)}) collective-permute-start(bf16[4,256,512]{2,1,0:T(8,128)(2,1)} %get-tuple-element.16), channel_id=1, source_target_pairs={{0,2},{1,3},{4,6},{5,7},{8,10},{9,11},{12,14},{13,15},{16,18},{17,... | collective-permute-start | bytes 3145736 | tf_op jit(solution)/shard_map/ppermute | solution.py:213
  19.5 0.0 collective-permute-start.1
  19.5 2.8 %collective-permute-start.2 = (bf16[4,256,512]{2,1,0:T(8,128)(2,1)}, bf16[4,256,512]{2,1,0:T(8,128)(2,1)S(1)}, u32[]{:S(2)}, u32[]{:S(2)}) collective-permute-start(bf16[4,256,512]{2,1,0:T(8,128)(2,1)} %get-tuple-element.19), channel_id=1, source_target_pairs={{0,131},{1,130},{4,135},{5,134},{8,139},{9,138},{12,143},{13,142},... | collective-permute-start | bytes 3145736 | tf_op jit(solution)/shard_map/ppermute | solution.py:214
  22.3 0.0 copy-done.2
  22.3 0.1 dynamic_slice.3
  22.4 5.0 %all-to-all-done.recv_ref = bf16[16,3,2,16,128]{4,3,2,1,0:T(8,128)(2,1)S(1)} async-done(((bf16[16,3,2,16,128]{4,3,2,1,0:T(8,128)(2,1)}), bf16[16,3,2,16,128]{4,3,2,1,0:T(8,128)(2,1)S(1)}, u32[]{:S(2)}, u32[]{:S(2)}) %all-to-all-start) | async-done | bytes 393248 | tf_op jit(solution)/shard_map/all_to_all | solution.py:219
  27.4 0.1 broadcast_in_dim.2.gain_ref
  27.5 5.4 %conv.1 = bf16[16,2,2,16,128]{4,3,2,1,0:T(8,128)(2,1)S(1)} custom-call(bf16[16,3,2,16,128]{4,3,2,1,0:T(8,128)(2,1)S(1)} %all-to-all-done.recv_ref, f32[16,128]{1,0:T(8,128)S(1)} %broadcast_in_dim.2.gain_ref), custom_call_target="tpu_custom_call" | custom-call | flops 536870912 | tf_op jit(solution)/shard_map/conv/pallas_call | solution.py:220
  32.8 18.2 %all_to_all.10 = bf16[32,2,16,128]{3,2,1,0:T(8,128)(2,1)S(1)} all-to-all(bf16[32,2,16,128]{3,2,1,0:T(8,128)(2,1)S(1)} %bitcast.5), channel_id=1, replica_groups={{0,2,16,18,32,34,48,50,64,66,80,82,96,98,112,114,128,130,144,146,160,16..., dimensions={0} | all-to-all | bytes 524288 | tf_op jit(solution)/shard_map/all_to_all | solution.py:236
  51.1 0.0 collective-permute-start.3
  51.1 0.0 collective-permute-done.ring_w
  51.1 2.0 %mine_terms.1 = (f32[256,512]{1,0:T(8,128)S(1)}, f32[256,512]{1,0:T(8,128)S(1)}, f32[256,512]{1,0:T(8,128)S(1)}, f32[256,512]{1,0:T(8,128)S(1)}) custom-call(s32[1]{0:T(128)} %bitcast.place_ref, bf16[4,256,512]{2,1,0:T(8,128)(2,1)S(1)} %get-tuple-element.15.own_w, bf16[4,256,512]{2,1,0:T(8,128)(2,1)} %collective-permute-done.ring_w, ...), custom_call_target="tpu_custom_call" | custom-call | flops 536870912 | bytes 1048576 | tf_op jit(solution)/shard_map/mine_terms/pallas_call | solution.py:144
  53.1 0.0 collective-permute-done.1.core_w
  53.1 0.0 collective-permute-done.2.diag_w
  53.1 0.0 collective-permute-done.3.rows_ref
  53.1 0.4 far_term.1
  53.5 1.5 %collective-permute-start.4 = (bf16[256,512]{1,0:T(8,128)(2,1)S(1)}, bf16[256,512]{1,0:T(8,128)(2,1)S(1)}, u32[]{:S(2)}, u32[]{:S(2)}) collective-permute-start(bf16[256,512]{1,0:T(8,128)(2,1)S(1)} %get-tuple-element.24.after), channel_id=1, source_target_pairs={{0,8},{1,9},{2,10},{3,11},{4,12},{5,13},{6,14},{7,15},{8,0},{9,1},... | collective-permute-start | bytes 786440 | tf_op jit(solution)/shard_map/ppermute | solution.py:245
  55.0 0.3 add_core.3.after
  55.3 0.3 add_core.4.after
  55.6 0.1 collective-permute-start.6
  55.7 3.2 %collective-permute-start.5 = (bf16[256,512]{1,0:T(8,128)(2,1)S(1)}, bf16[256,512]{1,0:T(8,128)(2,1)S(1)}, u32[]{:S(2)}, u32[]{:S(2)}) collective-permute-start(bf16[256,512]{1,0:T(8,128)(2,1)S(1)} %add_core.3.after), channel_id=1, source_target_pairs={{0,4},{1,5},{2,6},{3,7},{4,8},{5,9},{6,10},{7,11},{8,12},{9,13},{1... | collective-permute-start | bytes 786440 | tf_op jit(solution)/shard_map/ppermute | solution.py:246
  58.9 0.3 add_core.5.own
  59.2 5.0 %collective-permute-done.4.far = bf16[256,512]{1,0:T(8,128)(2,1)S(1)} collective-permute-done((bf16[256,512]{1,0:T(8,128)(2,1)S(1)}, bf16[256,512]{1,0:T(8,128)(2,1)S(1)}, u32[]{:S(2)}, u32[]{:S(2)}) %collective-permute-start.4) | collective-permute-done | bytes 262176 | tf_op jit(solution)/shard_map/ppermute | solution.py:245
  64.3 5.1 %collective-permute-done.6.down = bf16[256,512]{1,0:T(8,128)(2,1)S(1)} collective-permute-done((bf16[256,512]{1,0:T(8,128)(2,1)S(1)}, bf16[256,512]{1,0:T(8,128)(2,1)S(1)}, u32[]{:S(2)}, u32[]{:S(2)}) %collective-permute-start.6) | collective-permute-done | bytes 262176 | tf_op jit(solution)/shard_map/ppermute | solution.py:247
  69.4 0.0 collective-permute-done.5.up
  69.4 0.9 %sum.1 = bf16[512,256]{1,0:T(8,128)(2,1)} custom-call(f32[256,512]{1,0:T(8,128)S(1)} %two.1, bf16[256,512]{1,0:T(8,128)(2,1)S(1)} %collective-permute-done.5.up, bf16[256,512]{1,0:T(8,128)(2,1)S(1)} %collective-permute-done.6.down), custom_call_target="tpu_custom_call" | custom-call | tf_op jit(solution)/shard_map/sum/pallas_call | solution.py:256
  (1 shorter events, 0.0 us)
Async XLA Ops:
  0.0 22.3 %copy-start.2 = (f32[256]{0:T(256)S(1)}, f32[256]{0:T(256)}, u32[]{:S(2)}) copy-start(f32[256]{0:T(256)} %param.10) | copy-start | bytes 3076
  2.0 25.4 %all-to-all-start = ((bf16[16,3,2,16,128]{4,3,2,1,0:T(8,128)(2,1)}), bf16[16,3,2,16,128]{4,3,2,1,0:T(8,128)(2,1)S(1)}, u32[]{:S(2)}, u32[]{:S(2)}) async-start(bf16[16,3,2,16,128]{4,3,2,1,0:T(8,128)(2,1)} %pack.1.refs_1_), calls=%async_computation | async-start | bytes 786432 | tf_op jit(solution)/shard_map/all_to_all | solution.py:219
  13.2 2.2 %copy-start = (bf16[256,8192]{1,0:T(8,128)(2,1)S(1)}, bf16[256,8192]{1,0:T(8,128)(2,1)}, u32[]{:S(2)}) copy-start(bf16[256,8192]{1,0:T(8,128)(2,1)} %refs_0_.1) | copy-start | bytes 12582916
  15.4 1.0 %copy-start.1 = (bf16[16,3,2,16,128]{4,3,2,1,0:T(8,128)(2,1)S(1)}, bf16[16,3,2,16,128]{4,3,2,1,0:T(8,128)(2,1)}, u32[]{:S(2)}) copy-start(bf16[16,3,2,16,128]{4,3,2,1,0:T(8,128)(2,1)} %pack.1.refs_1_) | copy-start | bytes 1179652
  18.7 32.3 %collective-permute-start = (bf16[4,256,512]{2,1,0:T(8,128)(2,1)}, bf16[4,256,512]{2,1,0:T(8,128)(2,1)}, u32[]{:S(2)}, u32[]{:S(2)}) collective-permute-start(bf16[4,256,512]{2,1,0:T(8,128)(2,1)} %get-tuple-element.16), channel_id=1, source_target_pairs={{0,2},{1,3},{4,6},{5,7},{8,10},{9,11},{12,14},{13,15},{16,18},{17,... | collective-permute-start | bytes 3145736 | tf_op jit(solution)/shard_map/ppermute | solution.py:213
  19.5 33.6 %collective-permute-start.1 = (bf16[4,256,512]{2,1,0:T(8,128)(2,1)}, bf16[4,256,512]{2,1,0:T(8,128)(2,1)S(1)}, u32[]{:S(2)}, u32[]{:S(2)}) collective-permute-start(bf16[4,256,512]{2,1,0:T(8,128)(2,1)} %get-tuple-element.18), channel_id=1, source_target_pairs={{0,1},{1,0},{2,3},{3,2},{4,5},{5,4},{6,7},{7,6},{8,9},{9,8},{10,11... | collective-permute-start | bytes 3145736 | tf_op jit(solution)/shard_map/ppermute | solution.py:215
  19.5 33.6 %collective-permute-start.2 = (bf16[4,256,512]{2,1,0:T(8,128)(2,1)}, bf16[4,256,512]{2,1,0:T(8,128)(2,1)S(1)}, u32[]{:S(2)}, u32[]{:S(2)}) collective-permute-start(bf16[4,256,512]{2,1,0:T(8,128)(2,1)} %get-tuple-element.19), channel_id=1, source_target_pairs={{0,131},{1,130},{4,135},{5,134},{8,139},{9,138},{12,143},{13,142},... | collective-permute-start | bytes 3145736 | tf_op jit(solution)/shard_map/ppermute | solution.py:214
  51.1 2.0 %collective-permute-start.3 = (bf16[16,2,2,16,128]{4,3,2,1,0:T(8,128)(2,1)S(1)}, bf16[16,2,2,16,128]{4,3,2,1,0:T(8,128)(2,1)S(1)}, u32[]{:S(2)}, u32[]{:S(2)}) collective-permute-start(bf16[16,2,2,16,128]{4,3,2,1,0:T(8,128)(2,1)S(1)} %bitcast.3), channel_id=1, source_target_pairs={{0,1},{1,0},{2,3},{3,2},{4,5},{5,4},{6,7},{7,6},{8,9},{9,8},{10,11... | collective-permute-start | bytes 786440 | tf_op jit(solution)/shard_map/ppermute | solution.py:238
  53.5 10.7 %collective-permute-start.4 = (bf16[256,512]{1,0:T(8,128)(2,1)S(1)}, bf16[256,512]{1,0:T(8,128)(2,1)S(1)}, u32[]{:S(2)}, u32[]{:S(2)}) collective-permute-start(bf16[256,512]{1,0:T(8,128)(2,1)S(1)} %get-tuple-element.24.after), channel_id=1, source_target_pairs={{0,8},{1,9},{2,10},{3,11},{4,12},{5,13},{6,14},{7,15},{8,0},{9,1},... | collective-permute-start | bytes 786440 | tf_op jit(solution)/shard_map/ppermute | solution.py:245
  55.6 13.8 %collective-permute-start.6 = (bf16[256,512]{1,0:T(8,128)(2,1)S(1)}, bf16[256,512]{1,0:T(8,128)(2,1)S(1)}, u32[]{:S(2)}, u32[]{:S(2)}) collective-permute-start(bf16[256,512]{1,0:T(8,128)(2,1)S(1)} %add_core.4.after), channel_id=1, source_target_pairs={{0,12},{1,13},{2,14},{3,15},{4,0},{5,1},{6,2},{7,3},{8,4},{9,5},{1... | collective-permute-start | bytes 786440 | tf_op jit(solution)/shard_map/ppermute | solution.py:247
  55.7 13.7 %collective-permute-start.5 = (bf16[256,512]{1,0:T(8,128)(2,1)S(1)}, bf16[256,512]{1,0:T(8,128)(2,1)S(1)}, u32[]{:S(2)}, u32[]{:S(2)}) collective-permute-start(bf16[256,512]{1,0:T(8,128)(2,1)S(1)} %add_core.3.after), channel_id=1, source_target_pairs={{0,4},{1,5},{2,6},{3,7},{4,8},{5,9},{6,10},{7,11},{8,12},{9,13},{1... | collective-permute-start | bytes 786440 | tf_op jit(solution)/shard_map/ppermute | solution.py:246

commit v3 on v2

v3 whole, which is shorter than its diff:
```python
import functools

import jax
import jax.numpy as jnp
from jax import lax
from jax.experimental import pallas as pl
from jax.experimental.pallas import tpu as pltpu
from jax.sharding import PartitionSpec as P

N_SEQ, N_X, N_CHAN = 16, 4, 16
LANES = 128
VMEM = pl.BlockSpec(memory_space=pltpu.VMEM)
SMEM = pl.BlockSpec(memory_space=pltpu.SMEM)
ANY = pl.BlockSpec(memory_space=pl.ANY)


def chan_perm(dx, dy, dk):
    return [
        ((x * 2 + y) * 2 + k, ((x + dx) % N_X * 2 + (y ^ dy)) * 2 + (k ^ dk))
        for x in range(N_X)
        for y in range(2)
        for k in range(2)
    ]


def ring_y_perm(step, dk):
    pairs = []
    for y in range(4):
        to = (y + step) % 4
        for z in range(8):
            for x in range(N_X):
                for k in range(2):
                    source = (y // 2 * 8 + z) * N_CHAN + (x * 2 + y % 2) * 2 + k
                    target = (to // 2 * 8 + z) * N_CHAN + (x * 2 + to % 2) * 2 + (k ^ dk)
                    pairs.append((source, target))
    return pairs


def seq_y_groups():
    return [
        [seq * N_CHAN + (x * 2 + y) * 2 + k for seq in range(N_SEQ) for y in range(2)]
        for x in range(N_X)
        for k in range(2)
    ]


def pack_kernel(query_ref, key_ref, value_ref, taps_ref, out_ref, token_ref):
    for dst in range(N_SEQ):
        rows = slice(16 * dst, 16 * dst + 16)
        for half in range(2):
            cols = slice(LANES * half, LANES * half + LANES)
            gated = key_ref[rows, cols].astype(jnp.float32) * value_ref[rows, cols].astype(jnp.float32)
            out_ref[dst, 0, half] = gated.astype(jnp.bfloat16)
            out_ref[dst, 1, half] = taps_ref[rows, cols].astype(jnp.bfloat16)
            out_ref[dst, 2, half] = query_ref[rows, cols]
    token_ref[...] = jnp.zeros_like(token_ref)


def conv_kernel(recv_ref, gain_ref, out_ref, xs, hs, ys, xpad, done, sems):
    for s in range(N_SEQ):
        for half in range(2):
            rows = slice(32 * s + 16 * half, 32 * s + 16 * half + 16)
            xs[rows, :] = recv_ref[s, 0, half].astype(jnp.float32)
            hs[rows, :] = recv_ref[s, 1, half].astype(jnp.float32)
    for b in range(2):
        xpad[b, 0:32, :] = jnp.zeros((32, LANES), jnp.float32)
    lane = lax.broadcasted_iota(jnp.int32, (8, LANES), 1)
    row = lax.broadcasted_iota(jnp.int32, (8, LANES), 0)
    inside = [lane + row < LANES - 8 * g for g in range(16)]

    def body(p, carry):
        for b in range(2):
            xpad[b, 32:64, :] = xs[pl.ds(2 * p + b, 32, stride=16), :]
        before = [jnp.zeros((8, LANES), jnp.float32)] * 2
        total = jnp.zeros((64, 2 * LANES), jnp.float32)
        for d in range(32):
            shifted = jnp.concatenate([xpad[b, 32 - d : 64 - d, :] for b in range(2)], 0).astype(jnp.bfloat16)
            blocks = []
            for b in range(2):
                taps = jnp.broadcast_to(hs[pl.ds(16 * d + 2 * p + b, 1), :], (8, LANES))
                tiles = [
                    pltpu.roll(jnp.where(inside[g], taps, before[b]), 8 * g, 1, stride=1, stride_axis=0)
                    for g in range(16)
                ]
                before[b] = taps
                blocks.append(jnp.concatenate(tiles, 0).astype(jnp.bfloat16))
            total += jnp.dot(shifted, jnp.concatenate(blocks, 1), preferred_element_type=jnp.float32)
        ys[pl.ds(2 * p, 32, stride=16), :] = total[:32, :LANES]
        ys[pl.ds(2 * p + 1, 32, stride=16), :] = total[32:, LANES:]
        return carry

    lax.fori_loop(0, 8, body, 0, unroll=8)
    for s in range(N_SEQ):
        for half in range(2):
            rows = slice(32 * s + 16 * half, 32 * s + 16 * half + 16)
            total = ys[rows, :] + gain_ref[...] * xs[rows, :]
            done[s, half] = (recv_ref[s, 2, half].astype(jnp.float32) * total).astype(jnp.bfloat16)
    copies = [pltpu.make_async_copy(done, out_ref.at[:, y], sems.at[y]) for y in range(2)]
    for copy in copies:
        copy.start()
    for copy in copies:
        copy.wait()


def slice_kernel(parts, place_ref, after_ref, weight_ref, *refs):
    outs, held, in_sems, out_sems = refs[: len(parts)], refs[len(parts) : -2], refs[-2], refs[-1]
    loads, stores = [], []
    for number, (other, steps) in enumerate(parts):
        for slot, n in enumerate(steps):
            column = (place_ref[0] // 4 + n) % N_X * 4 + ((place_ref[0] % 4) ^ other)
            source = weight_ref.at[:, pl.ds(pl.multiple_of(column * 512, 512), 512)]
            loads.append((number, pltpu.make_async_copy(source, held[number].at[slot], in_sems.at[number, slot])))
            loads[-1][1].start()
    for number in range(len(parts)):
        for at, load in loads:
            if at == number:
                load.wait()
        stores.append(pltpu.make_async_copy(held[number], outs[number], out_sems.at[number]))
        stores[-1].start()
    for store in stores:
        store.wait()


def weight_slices(parts, limit, weight, place, after):
    shapes = [(len(steps), 256, 512) for other, steps in parts]
    return pl.pallas_call(
        functools.partial(slice_kernel, parts),
        in_specs=[SMEM, ANY, ANY],
        out_specs=[ANY] * len(parts),
        out_shape=[jax.ShapeDtypeStruct(shape, jnp.bfloat16) for shape in shapes],
        scratch_shapes=[pltpu.VMEM(shape, jnp.bfloat16) for shape in shapes]
        + [pltpu.SemaphoreType.DMA((len(parts), N_X)), pltpu.SemaphoreType.DMA((len(parts),))],
        cost_estimate=pl.CostEstimate(flops=0, bytes_accessed=len(parts) * 2**20, transcendentals=0),
        compiler_params=pltpu.CompilerParams(vmem_limit_bytes=limit * 2**20),
        name="weight_slices",
    )(place, after, weight)


def by_position(rows_ref, y):
    halves = [jnp.concatenate([rows_ref[src, y, half] for src in range(N_SEQ)], 0) for half in range(2)]
    return jnp.concatenate([half.astype(jnp.float32).T.astype(jnp.bfloat16) for half in halves], 0)


def product(rows, first, second):
    total = jnp.dot(rows[:, :256], first, preferred_element_type=jnp.float32)
    return total + jnp.dot(rows[:, 256:], second, preferred_element_type=jnp.float32)


def mine_kernel(place_ref, own_w, ring_w, rows_ref, rows_out, out_ref):
    y = place_ref[0] // 2 % 2
    rows_out[:, :256] = by_position(rows_ref, y)
    rows_out[:, 256:] = by_position(rows_ref, 1 - y)
    out_ref[...] = product(rows_out, own_w[...], ring_w[2])


def far_kernel(place_ref, mine, core_w, diag_w, rows_ref, rows_out, out_ref):
    y = place_ref[0] // 2 % 2
    rows_out[:, :256] = by_position(rows_ref, y)
    rows_out[:, 256:] = by_position(rows_ref, 1 - y)
    out_ref[...] = (mine[...] + product(rows_out, core_w[2], diag_w[2])).astype(jnp.bfloat16)


def near_kernel(n, own_w, ring_w, core_w, diag_w, mine_r, core_r, after, out_ref):
    total = product(mine_r, own_w[...], ring_w[n]) + product(core_r, core_w[n], diag_w[n])
    out_ref[...] = total.astype(out_ref.dtype)


def two_kernel(own, far, out_ref):
    out_ref[...] = own[...] + far[...].astype(jnp.float32)


def sum_kernel(two, up, down, out_ref):
    total = two[...] + up[...].astype(jnp.float32) + down[...].astype(jnp.float32)
    out_ref[...] = total.T.astype(jnp.bfloat16)


def gain_kernel(gain_ref, after, out_ref):
    out_ref[...] = gain_ref[...]


def in_vmem(kernel, in_specs, outs, name, flops):
    return pl.pallas_call(
        kernel,
        in_specs=in_specs,
        out_specs=[VMEM] * len(outs),
        out_shape=outs,
        cost_estimate=pl.CostEstimate(flops=flops, bytes_accessed=2**20, transcendentals=0),
        compiler_params=pltpu.CompilerParams(vmem_limit_bytes=8 * 2**20),
        name=name,
    )


def local(query_act, key_act, value_act, filter_taps, skip_gain, out_weight):
    chan = lax.axis_index("chan")
    both = ("seq", "chan")
    send, token = pl.pallas_call(
        pack_kernel,
        out_shape=[
            jax.ShapeDtypeStruct((N_SEQ, 3, 2, 16, LANES), jnp.bfloat16),
            jax.ShapeDtypeStruct((8, LANES), jnp.float32),
        ],
        in_specs=[VMEM] * 4,
        out_specs=[VMEM] * 2,
        name="pack",
    )(query_act, key_act, value_act, filter_taps)
    place = jnp.reshape(chan, (1,)).astype(jnp.int32)
    every = (0, 1, 2, 3)
    ring_w, diag_w, core_w = weight_slices(((2, every), (3, every), (1, every)), 59, out_weight, place, token)
    own_w = weight_slices(tuple((0, (n,)) for n in every), 59, out_weight, place, token)
    own_w = [jnp.reshape(part, (256, 512)) for part in own_w]
    ring_w = lax.ppermute(ring_w, both, ring_y_perm(1, 0))
    diag_w = lax.ppermute(diag_w, both, ring_y_perm(-1, 1))
    core_w = lax.ppermute(core_w, "chan", chan_perm(0, 0, 1))

    gain = lax.dynamic_slice(skip_gain, (16 * lax.axis_index("seq"),), (16,))
    gain = jnp.broadcast_to(gain[:, None], (16, LANES))
    tile = jax.ShapeDtypeStruct((16, LANES), jnp.float32)
    (gain,) = in_vmem(gain_kernel, [VMEM, ANY], [tile], "gain", 0)(gain, own_w[2])
    recv = lax.all_to_all(send, "seq", 0, 0, tiled=True)
    rows = pl.pallas_call(
        conv_kernel,
        out_shape=jax.ShapeDtypeStruct((N_SEQ, 2, 2, 16, LANES), jnp.bfloat16),
        in_specs=[VMEM, VMEM],
        out_specs=ANY,
        scratch_shapes=[pltpu.VMEM((512, LANES), jnp.float32)] * 3
        + [
            pltpu.VMEM((2, 64, LANES), jnp.float32),
            pltpu.VMEM((N_SEQ, 2, 16, LANES), jnp.bfloat16),
            pltpu.SemaphoreType.DMA((2,)),
        ],
        cost_estimate=pl.CostEstimate(flops=2 * 16 * 4096 * 4096, bytes_accessed=0, transcendentals=0),
        compiler_params=pltpu.CompilerParams(vmem_limit_bytes=8 * 2**20),
        name="conv",
    )(recv, gain)
    rows = jnp.reshape(rows, (2 * N_SEQ, 2, 16, LANES))
    rows = lax.all_to_all(rows, both, 0, 0, axis_index_groups=seq_y_groups(), tiled=True)
    rows = jnp.reshape(rows, (N_SEQ, 2, 2, 16, LANES))
    core_rows = lax.ppermute(rows, "chan", chan_perm(0, 0, 1))
    flops = 2 * 256 * 512 * 512
    narrow, wide = jax.ShapeDtypeStruct((256, 512), jnp.bfloat16), jax.ShapeDtypeStruct((256, 512), jnp.float32)
    mine_r, mine = in_vmem(mine_kernel, [SMEM] + [VMEM] * 3, [narrow, wide], "mine", flops)(
        place, own_w[2], ring_w, rows
    )
    core_r, far = in_vmem(far_kernel, [SMEM] + [VMEM] * 4, [narrow] * 2, "far", flops)(
        place, mine, core_w, diag_w, core_rows
    )

    def near(n, after, kind):
        call = in_vmem(functools.partial(near_kernel, n), [VMEM] * 6 + [ANY], [kind], "near", 2 * flops)
        return call(own_w[n], ring_w, core_w, diag_w, mine_r, core_r, after)[0]

    up = near(1, far, narrow)
    down = near(3, up, narrow)
    own = near(0, down, wide)
    far = lax.ppermute(far, "chan", chan_perm(2, 0, 0))
    up = lax.ppermute(up, "chan", chan_perm(1, 0, 0))
    down = lax.ppermute(down, "chan", chan_perm(-1, 0, 0))
    (two,) = in_vmem(two_kernel, [VMEM] * 2, [wide], "two", 0)(own, far)
    out = jax.ShapeDtypeStruct((512, 256), jnp.bfloat16)
    return in_vmem(sum_kernel, [VMEM] * 3, [out], "sum", 0)(two, up, down)[0]


def solution(mesh):
    placed = (
        P("chan", "seq"),
        P("chan", "seq"),
        P("chan", "seq"),
        P("chan", "seq"),
        P("chan"),
        P("chan", None),
    )
    return jax.shard_map(
        local, mesh=mesh, in_specs=placed, out_specs=P("chan", "seq"), check_vma=False
    )
```

time: 71.6 us -> 70.2 us (0.980)
  local copies, waits for them, and re-layouts: 3.33 us -> 2.07 us
  starting transfers between devices: 19.6 us -> 18.5 us
  Pallas kernels: 13.8 us -> 14.6 us
    ppermute x1, waiting for transfers between devices: 5.14 us -> 2.15 us  [local(): down = lax.ppermute(down, 'chan', chan_perm(-1, 0, 0))]
    ppermute x1, waiting for transfers between devices: 0.01 us -> 2.84 us  [local(): up = lax.ppermute(up, 'chan', chan_perm(1, 0, 0))]
    pallas_call x9 -> x11, Pallas kernels: 8.47 us -> 9.95 us  [the longest x2 5.08 us: weight_slices(): pl.pallas_call(functools.partial(slice_kernel, parts), in_specs=[SMEM, AN...]
    unnamed x6 -> x12, local copies, waits for them, and re-layouts: 3.18 us -> 1.92 us
    ppermute x1, starting transfers between devices: 3.22 us -> 2.17 us  [local(): up = lax.ppermute(up, 'chan', chan_perm(1, 0, 0))]
  transfers between devices with their start and end apart: 8 -> 8, of which waited for: 3 -> 5; matrix products, arithmetic and copies ran while one was open for 0% -> 0% of each run, Pallas kernels for 15% -> 17%
where the time goes in v3:
time: 70.2 us; the launch traced here: 68.8 us
  starting transfers between devices  18.5 us (26%)
  blocking collectives  18.2 us (26%)
  waiting for transfers between devices  15.3 us (22%)
  Pallas kernels  14.6 us (21%)
  local copies, waits for them, and re-layouts  2.07 us (3%)
    all_to_all x1, blocking collectives, local(): lax.all_to_all(rows, both, 0, 0, axis_index_groups=seq_y_groups(), tiled=...  18.2 us
    all_to_all x1, starting transfers between devices, local(): recv = lax.all_to_all(send, 'seq', 0, 0, tiled=True)  11.2 us
    ppermute x1, waiting for transfers between devices, local(): far = lax.ppermute(far, 'chan', chan_perm(2, 0, 0))  5.62 us
    pallas_call x2, Pallas kernels, weight_slices(): pl.pallas_call(functools.partial(slice_kernel, parts), in_specs=[SMEM, AN...  5.08 us
    pallas_call x1, Pallas kernels, local(): pl.pallas_call(conv_kernel, out_shape=jax.ShapeDtypeStruct((N_SEQ, 2, 2,...  4.66 us
    all_to_all x1, waiting for transfers between devices, local(): recv = lax.all_to_all(send, 'seq', 0, 0, tiled=True)  4.44 us
    ppermute x1, waiting for transfers between devices, local(): up = lax.ppermute(up, 'chan', chan_perm(1, 0, 0))  2.84 us
    ppermute x1, starting transfers between devices, local(): diag_w = lax.ppermute(diag_w, both, ring_y_perm(-1, 1))  2.79 us
  transfers between devices with their start and end apart: 8, of which 5 were waited for; matrix products, arithmetic and copies ran while one was open for 0% of the time, Pallas kernels for 17%

profile of v3, /device:TPU:6, one launch (start us, length us, event | category | flops | bytes accessed | tf_op | source)
XLA Modules:
  0.0 68.8 jit_solution(10829385948534750981)
XLA Ops:
  0.0 2.0 %pack.1 = (bf16[16,3,2,16,128]{4,3,2,1,0:T(8,128)(2,1)}, f32[8,128]{1,0:T(8,128)}) custom-call(bf16[256,256]{1,0:T(8,128)(2,1)} %query_ref.1, bf16[256,256]{1,0:T(8,128)(2,1)} %key_ref.1, bf16[256,256]{1,0:T(8,128)(2,1)} %value_ref.1, f32[256,256]{1,0:T(8,128)} %taps_ref.1), custom_call_target="tpu_custom_call" | custom-call | tf_op jit(solution)/shard_map/pack/pallas_call | solution.py:196
  2.0 11.2 %all-to-all-start = ((bf16[16,3,2,16,128]{4,3,2,1,0:T(8,128)(2,1)}), bf16[16,3,2,16,128]{4,3,2,1,0:T(8,128)(2,1)S(1)}, u32[]{:S(2)}, u32[]{:S(2)}) async-start(bf16[16,3,2,16,128]{4,3,2,1,0:T(8,128)(2,1)} %get-tuple-element.24), calls=%async_computation | async-start | bytes 786432 | tf_op jit(solution)/shard_map/all_to_all | solution.py:219
  13.2 0.0 copy-start.5
  13.2 3.0 %weight_slices.3 = (bf16[4,256,512]{2,1,0:T(8,128)(2,1)}, bf16[4,256,512]{2,1,0:T(8,128)(2,1)}, bf16[4,256,512]{2,1,0:T(8,128)(2,1)}) custom-call(s32[1]{0:T(128)} %bitcast.place_ref, f32[8,128]{1,0:T(8,128)} %get-tuple-element.18.after_ref, bf16[256,8192]{1,0:T(8,128)(2,1)} %weight_ref.3), custom_call_target="tpu_custom_call" | custom-call | bytes 3145728 | tf_op jit(solution)/shard_map/weight_slices/pallas_call | solution.py:126
  16.2 0.8 %collective-permute-start = (bf16[4,256,512]{2,1,0:T(8,128)(2,1)}, bf16[4,256,512]{2,1,0:T(8,128)(2,1)S(1)}, u32[]{:S(2)}, u32[]{:S(2)}) collective-permute-start(bf16[4,256,512]{2,1,0:T(8,128)(2,1)} %get-tuple-element.20), channel_id=1, source_target_pairs={{0,2},{1,3},{4,6},{5,7},{8,10},{9,11},{12,14},{13,15},{16,18},{17,... | collective-permute-start | bytes 3145736 | tf_op jit(solution)/shard_map/ppermute | solution.py:211
  17.0 0.0 collective-permute-start.1
  17.0 2.8 %collective-permute-start.2 = (bf16[4,256,512]{2,1,0:T(8,128)(2,1)}, bf16[4,256,512]{2,1,0:T(8,128)(2,1)S(1)}, u32[]{:S(2)}, u32[]{:S(2)}) collective-permute-start(bf16[4,256,512]{2,1,0:T(8,128)(2,1)} %get-tuple-element.22), channel_id=1, source_target_pairs={{0,131},{1,130},{4,135},{5,134},{8,139},{9,138},{12,143},{13,142},... | collective-permute-start | bytes 3145736 | tf_op jit(solution)/shard_map/ppermute | solution.py:212
  19.8 2.1 %weight_slices.2 = (bf16[1,256,512]{2,1,0:T(8,128)(2,1)}, bf16[1,256,512]{2,1,0:T(8,128)(2,1)}, bf16[1,256,512]{2,1,0:T(8,128)(2,1)}, bf16[1,256,512]{2,1,0:T(8,128)(2,1)}) custom-call(s32[1]{0:T(128)} %bitcast.place_ref, f32[8,128]{1,0:T(8,128)} %get-tuple-element.18.after_ref, bf16[256,8192]{1,0:T(8,128)(2,1)} %weight_ref.3), custom_call_target="tpu_custom_call" | custom-call | bytes 4194304 | tf_op jit(solution)/shard_map/weight_slices/pallas_call | solution.py:126
  21.9 0.0 copy-done.5
  21.9 0.1 dynamic_slice.3
  21.9 0.1 broadcast_in_dim.2.gain_ref
  22.0 0.0 copy-start
  22.0 0.9 %copy-done = bf16[1,256,512]{2,1,0:T(8,128)(2,1)S(1)} copy-done((bf16[1,256,512]{2,1,0:T(8,128)(2,1)S(1)}, bf16[1,256,512]{2,1,0:T(8,128)(2,1)}, u32[]{:S(2)}) %copy-start) | copy-done | bytes 262168
  23.0 4.4 %all-to-all-done.recv_ref = bf16[16,3,2,16,128]{4,3,2,1,0:T(8,128)(2,1)S(1)} async-done(((bf16[16,3,2,16,128]{4,3,2,1,0:T(8,128)(2,1)}), bf16[16,3,2,16,128]{4,3,2,1,0:T(8,128)(2,1)S(1)}, u32[]{:S(2)}, u32[]{:S(2)}) %all-to-all-start) | async-done | bytes 393248 | tf_op jit(solution)/shard_map/all_to_all | solution.py:219
  27.4 0.0 copy-start.4
  27.4 4.7 %conv.1 = bf16[16,2,2,16,128]{4,3,2,1,0:T(8,128)(2,1)S(1)} custom-call(bf16[16,3,2,16,128]{4,3,2,1,0:T(8,128)(2,1)S(1)} %all-to-all-done.recv_ref, f32[16,128]{1,0:T(8,128)S(1)} %gain.1.gain_ref), custom_call_target="tpu_custom_call" | custom-call | flops 536870912 | tf_op jit(solution)/shard_map/conv/pallas_call | solution.py:220
  32.1 18.2 %all_to_all.10 = bf16[32,2,16,128]{3,2,1,0:T(8,128)(2,1)S(1)} all-to-all(bf16[32,2,16,128]{3,2,1,0:T(8,128)(2,1)S(1)} %bitcast.14), channel_id=1, replica_groups={{0,2,16,18,32,34,48,50,64,66,80,82,96,98,112,114,128,130,144,146,160,16..., dimensions={0} | all-to-all | bytes 524288 | tf_op jit(solution)/shard_map/all_to_all | solution.py:236
  50.3 0.0 collective-permute-start.3
  50.3 0.0 collective-permute-done.ring_w
  50.3 0.0 copy-start.1
  50.3 0.9 %copy-done.1 = bf16[1,256,512]{2,1,0:T(8,128)(2,1)S(1)} copy-done((bf16[1,256,512]{2,1,0:T(8,128)(2,1)S(1)}, bf16[1,256,512]{2,1,0:T(8,128)(2,1)}, u32[]{:S(2)}) %copy-start.1) | copy-done | bytes 262168
  51.3 0.0 copy-start.3
  51.3 0.4 mine.1
  51.6 0.0 collective-permute-done.1.core_w
  51.6 0.0 collective-permute-done.2.diag_w
  51.7 0.2 collective-permute-done.3.rows_ref
  51.9 0.4 far.1
  52.2 1.5 %collective-permute-start.4 = (bf16[256,512]{1,0:T(8,128)(2,1)S(1)}, bf16[256,512]{1,0:T(8,128)(2,1)S(1)}, u32[]{:S(2)}, u32[]{:S(2)}) collective-permute-start(bf16[256,512]{1,0:T(8,128)(2,1)S(1)} %get-tuple-element.30.after), channel_id=1, source_target_pairs={{0,8},{1,9},{2,10},{3,11},{4,12},{5,13},{6,14},{7,15},{8,0},{9,1},... | collective-permute-start | bytes 786440 | tf_op jit(solution)/shard_map/ppermute | solution.py:255
  53.7 0.0 copy-done.4
  53.7 0.0 copy-start.2
  53.7 0.4 near.3.after
  54.2 2.2 %collective-permute-start.5 = (bf16[256,512]{1,0:T(8,128)(2,1)S(1)}, bf16[256,512]{1,0:T(8,128)(2,1)S(1)}, u32[]{:S(2)}, u32[]{:S(2)}) collective-permute-start(bf16[256,512]{1,0:T(8,128)(2,1)S(1)} %near.3.after), channel_id=1, source_target_pairs={{0,4},{1,5},{2,6},{3,7},{4,8},{5,9},{6,10},{7,11},{8,12},{9,13},{1... | collective-permute-start | bytes 786440 | tf_op jit(solution)/shard_map/ppermute | solution.py:256
  56.3 0.0 copy-done.3
  56.3 0.4 near.4.after
  56.8 0.1 collective-permute-start.6
  56.9 0.0 copy-done.2
  56.9 0.4 near.5.own
  57.3 5.6 %collective-permute-done.4.far = bf16[256,512]{1,0:T(8,128)(2,1)S(1)} collective-permute-done((bf16[256,512]{1,0:T(8,128)(2,1)S(1)}, bf16[256,512]{1,0:T(8,128)(2,1)S(1)}, u32[]{:S(2)}, u32[]{:S(2)}) %collective-permute-start.4) | collective-permute-done | bytes 262176 | tf_op jit(solution)/shard_map/ppermute | solution.py:255
  63.0 2.8 %collective-permute-done.5.up = bf16[256,512]{1,0:T(8,128)(2,1)S(1)} collective-permute-done((bf16[256,512]{1,0:T(8,128)(2,1)S(1)}, bf16[256,512]{1,0:T(8,128)(2,1)S(1)}, u32[]{:S(2)}, u32[]{:S(2)}) %collective-permute-start.5) | collective-permute-done | bytes 262176 | tf_op jit(solution)/shard_map/ppermute | solution.py:256
  65.8 2.2 %collective-permute-done.6.down = bf16[256,512]{1,0:T(8,128)(2,1)S(1)} collective-permute-done((bf16[256,512]{1,0:T(8,128)(2,1)S(1)}, bf16[256,512]{1,0:T(8,128)(2,1)S(1)}, u32[]{:S(2)}, u32[]{:S(2)}) %collective-permute-start.6) | collective-permute-done | bytes 262176 | tf_op jit(solution)/shard_map/ppermute | solution.py:257
  68.0 0.9 %sum.1 = bf16[512,256]{1,0:T(8,128)(2,1)} custom-call(f32[256,512]{1,0:T(8,128)S(1)} %two.1, bf16[256,512]{1,0:T(8,128)(2,1)S(1)} %collective-permute-done.5.up, bf16[256,512]{1,0:T(8,128)(2,1)S(1)} %collective-permute-done.6.down), custom_call_target="tpu_custom_call" | custom-call | bytes 1048576 | tf_op jit(solution)/shard_map/sum/pallas_call | solution.py:260
  (2 shorter events, 0.0 us)
Async XLA Ops:
  2.0 25.4 %all-to-all-start = ((bf16[16,3,2,16,128]{4,3,2,1,0:T(8,128)(2,1)}), bf16[16,3,2,16,128]{4,3,2,1,0:T(8,128)(2,1)S(1)}, u32[]{:S(2)}, u32[]{:S(2)}) async-start(bf16[16,3,2,16,128]{4,3,2,1,0:T(8,128)(2,1)} %get-tuple-element.24), calls=%async_computation | async-start | bytes 786432 | tf_op jit(solution)/shard_map/all_to_all | solution.py:219
  13.2 8.7 %copy-start.5 = (f32[256]{0:T(256)S(1)}, f32[256]{0:T(256)}, u32[]{:S(2)}) copy-start(f32[256]{0:T(256)} %param.10) | copy-start | bytes 3076
  16.2 34.1 %collective-permute-start = (bf16[4,256,512]{2,1,0:T(8,128)(2,1)}, bf16[4,256,512]{2,1,0:T(8,128)(2,1)S(1)}, u32[]{:S(2)}, u32[]{:S(2)}) collective-permute-start(bf16[4,256,512]{2,1,0:T(8,128)(2,1)} %get-tuple-element.20), channel_id=1, source_target_pairs={{0,2},{1,3},{4,6},{5,7},{8,10},{9,11},{12,14},{13,15},{16,18},{17,... | collective-permute-start | bytes 3145736 | tf_op jit(solution)/shard_map/ppermute | solution.py:211
  17.0 34.7 %collective-permute-start.1 = (bf16[4,256,512]{2,1,0:T(8,128)(2,1)}, bf16[4,256,512]{2,1,0:T(8,128)(2,1)S(1)}, u32[]{:S(2)}, u32[]{:S(2)}) collective-permute-start(bf16[4,256,512]{2,1,0:T(8,128)(2,1)} %get-tuple-element.21), channel_id=1, source_target_pairs={{0,1},{1,0},{2,3},{3,2},{4,5},{5,4},{6,7},{7,6},{8,9},{9,8},{10,11... | collective-permute-start | bytes 3145736 | tf_op jit(solution)/shard_map/ppermute | solution.py:213
  17.0 34.7 %collective-permute-start.2 = (bf16[4,256,512]{2,1,0:T(8,128)(2,1)}, bf16[4,256,512]{2,1,0:T(8,128)(2,1)S(1)}, u32[]{:S(2)}, u32[]{:S(2)}) collective-permute-start(bf16[4,256,512]{2,1,0:T(8,128)(2,1)} %get-tuple-element.22), channel_id=1, source_target_pairs={{0,131},{1,130},{4,135},{5,134},{8,139},{9,138},{12,143},{13,142},... | collective-permute-start | bytes 3145736 | tf_op jit(solution)/shard_map/ppermute | solution.py:212
  22.0 1.0 %copy-start = (bf16[1,256,512]{2,1,0:T(8,128)(2,1)S(1)}, bf16[1,256,512]{2,1,0:T(8,128)(2,1)}, u32[]{:S(2)}) copy-start(bf16[1,256,512]{2,1,0:T(8,128)(2,1)} %get-tuple-element.23) | copy-start | bytes 786436
  27.4 26.3 %copy-start.4 = (bf16[1,256,512]{2,1,0:T(8,128)(2,1)S(1)}, bf16[1,256,512]{2,1,0:T(8,128)(2,1)}, u32[]{:S(2)}) copy-start(bf16[1,256,512]{2,1,0:T(8,128)(2,1)} %get-tuple-element.29) | copy-start | bytes 786436
  50.3 1.5 %collective-permute-start.3 = (bf16[16,2,2,16,128]{4,3,2,1,0:T(8,128)(2,1)S(1)}, bf16[16,2,2,16,128]{4,3,2,1,0:T(8,128)(2,1)S(1)}, u32[]{:S(2)}, u32[]{:S(2)}) collective-permute-start(bf16[16,2,2,16,128]{4,3,2,1,0:T(8,128)(2,1)S(1)} %bitcast.9), channel_id=1, source_target_pairs={{0,1},{1,0},{2,3},{3,2},{4,5},{5,4},{6,7},{7,6},{8,9},{9,8},{10,11... | collective-permute-start | bytes 786440 | tf_op jit(solution)/shard_map/ppermute | solution.py:238
  50.3 1.0 %copy-start.1 = (bf16[1,256,512]{2,1,0:T(8,128)(2,1)S(1)}, bf16[1,256,512]{2,1,0:T(8,128)(2,1)}, u32[]{:S(2)}) copy-start(bf16[1,256,512]{2,1,0:T(8,128)(2,1)} %get-tuple-element.23) | copy-start | bytes 786436
  51.3 5.1 %copy-start.3 = (bf16[1,256,512]{2,1,0:T(8,128)(2,1)S(1)}, bf16[1,256,512]{2,1,0:T(8,128)(2,1)}, u32[]{:S(2)}) copy-start(bf16[1,256,512]{2,1,0:T(8,128)(2,1)} %get-tuple-element.28) | copy-start | bytes 786436
  52.2 10.7 %collective-permute-start.4 = (bf16[256,512]{1,0:T(8,128)(2,1)S(1)}, bf16[256,512]{1,0:T(8,128)(2,1)S(1)}, u32[]{:S(2)}, u32[]{:S(2)}) collective-permute-start(bf16[256,512]{1,0:T(8,128)(2,1)S(1)} %get-tuple-element.30.after), channel_id=1, source_target_pairs={{0,8},{1,9},{2,10},{3,11},{4,12},{5,13},{6,14},{7,15},{8,0},{9,1},... | collective-permute-start | bytes 786440 | tf_op jit(solution)/shard_map/ppermute | solution.py:255
  53.7 3.1 %copy-start.2 = (bf16[1,256,512]{2,1,0:T(8,128)(2,1)S(1)}, bf16[1,256,512]{2,1,0:T(8,128)(2,1)}, u32[]{:S(2)}) copy-start(bf16[1,256,512]{2,1,0:T(8,128)(2,1)} %get-tuple-element.19) | copy-start | bytes 786436
  54.2 11.7 %collective-permute-start.5 = (bf16[256,512]{1,0:T(8,128)(2,1)S(1)}, bf16[256,512]{1,0:T(8,128)(2,1)S(1)}, u32[]{:S(2)}, u32[]{:S(2)}) collective-permute-start(bf16[256,512]{1,0:T(8,128)(2,1)S(1)} %near.3.after), channel_id=1, source_target_pairs={{0,4},{1,5},{2,6},{3,7},{4,8},{5,9},{6,10},{7,11},{8,12},{9,13},{1... | collective-permute-start | bytes 786440 | tf_op jit(solution)/shard_map/ppermute | solution.py:256
  56.8 11.2 %collective-permute-start.6 = (bf16[256,512]{1,0:T(8,128)(2,1)S(1)}, bf16[256,512]{1,0:T(8,128)(2,1)S(1)}, u32[]{:S(2)}, u32[]{:S(2)}) collective-permute-start(bf16[256,512]{1,0:T(8,128)(2,1)S(1)} %near.4.after), channel_id=1, source_target_pairs={{0,12},{1,13},{2,14},{3,15},{4,0},{5,1},{6,2},{7,3},{8,4},{9,5},{1... | collective-permute-start | bytes 786440 | tf_op jit(solution)/shard_map/ppermute | solution.py:257

commit v4 on v3

--- a/solution.py
+++ b/solution.py
@@ -56,7 +56,7 @@
     token_ref[...] = jnp.zeros_like(token_ref)
 
 
-def conv_kernel(recv_ref, gain_ref, out_ref, xs, hs, ys, xpad, done, sems):
+def conv_kernel(recv_ref, gain_ref, out_ref, xs, hs, ys, xpad):
     for s in range(N_SEQ):
         for half in range(2):
             rows = slice(32 * s + 16 * half, 32 * s + 16 * half + 16)
@@ -94,12 +94,9 @@
         for half in range(2):
             rows = slice(32 * s + 16 * half, 32 * s + 16 * half + 16)
             total = ys[rows, :] + gain_ref[...] * xs[rows, :]
-            done[s, half] = (recv_ref[s, 2, half].astype(jnp.float32) * total).astype(jnp.bfloat16)
-    copies = [pltpu.make_async_copy(done, out_ref.at[:, y], sems.at[y]) for y in range(2)]
-    for copy in copies:
-        copy.start()
-    for copy in copies:
-        copy.wait()
+            gated = (recv_ref[s, 2, half].astype(jnp.float32) * total).astype(jnp.bfloat16)
+            out_ref[s, 0, half] = gated
+            out_ref[s, 1, half] = gated
 
 
 def slice_kernel(parts, place_ref, after_ref, weight_ref, *refs):
@@ -153,25 +150,40 @@
     out_ref[...] = product(rows_out, own_w[...], ring_w[2])
 
 
-def far_kernel(place_ref, mine, core_w, diag_w, rows_ref, rows_out, out_ref):
+def far_kernel(place_ref, mine, core_w, diag_w, rows_ref, rows_out, first_out, second_out):
     y = place_ref[0] // 2 % 2
     rows_out[:, :256] = by_position(rows_ref, y)
     rows_out[:, 256:] = by_position(rows_ref, 1 - y)
-    out_ref[...] = (mine[...] + product(rows_out, core_w[2], diag_w[2])).astype(jnp.bfloat16)
-
-
-def near_kernel(n, own_w, ring_w, core_w, diag_w, mine_r, core_r, after, out_ref):
+    total = (mine[...] + product(rows_out, core_w[2], diag_w[2])).astype(jnp.bfloat16)
+    first_out[...] = total[:LANES, :]
+    second_out[...] = total[LANES:, :]
+
+
+def near_kernel(n, own_w, ring_w, core_w, diag_w, mine_r, core_r, after, first_out, second_out):
     total = product(mine_r, own_w[...], ring_w[n]) + product(core_r, core_w[n], diag_w[n])
-    out_ref[...] = total.astype(out_ref.dtype)
-
-
-def two_kernel(own, far, out_ref):
-    out_ref[...] = own[...] + far[...].astype(jnp.float32)
-
-
-def sum_kernel(two, up, down, out_ref):
-    total = two[...] + up[...].astype(jnp.float32) + down[...].astype(jnp.float32)
-    out_ref[...] = total.T.astype(jnp.bfloat16)
+    first_out[...] = total[:LANES, :].astype(first_out.dtype)
+    second_out[...] = total[LANES:, :].astype(second_out.dtype)
+
+
+def relay_kernel(near, arrived, out_ref):
+    out_ref[...] = (near[...] + arrived[...].astype(jnp.float32)).astype(jnp.bfloat16)
+
+
+def two_kernel(own_a, own_b, above, below, out_ref):
+    out_ref[:LANES, :] = own_a[...] + above[...].astype(jnp.float32)
+    out_ref[LANES:, :] = own_b[...] + below[...].astype(jnp.float32)
+
+
+def sum_kernel(two, below, above, out_ref, held, sems):
+    stores = []
+    for part in range(4):
+        at = slice(LANES * part, LANES * part + LANES)
+        held[at, :LANES] = (two[:LANES, at] + below[:, at].astype(jnp.float32)).T.astype(jnp.bfloat16)
+        held[at, LANES:] = (two[LANES:, at] + above[:, at].astype(jnp.float32)).T.astype(jnp.bfloat16)
+        stores.append(pltpu.make_async_copy(held.at[at], out_ref.at[at], sems.at[part]))
+        stores[-1].start()
+    for store in stores:
+        store.wait()
 
 
 def gain_kernel(gain_ref, after, out_ref):
@@ -221,13 +233,8 @@
         conv_kernel,
         out_shape=jax.ShapeDtypeStruct((N_SEQ, 2, 2, 16, LANES), jnp.bfloat16),
         in_specs=[VMEM, VMEM],
-        out_specs=ANY,
-        scratch_shapes=[pltpu.VMEM((512, LANES), jnp.float32)] * 3
-        + [
-            pltpu.VMEM((2, 64, LANES), jnp.float32),
-            pltpu.VMEM((N_SEQ, 2, 16, LANES), jnp.bfloat16),
-            pltpu.SemaphoreType.DMA((2,)),
-        ],
+        out_specs=VMEM,
+        scratch_shapes=[pltpu.VMEM((512, LANES), jnp.float32)] * 3 + [pltpu.VMEM((2, 64, LANES), jnp.float32)],
         cost_estimate=pl.CostEstimate(flops=2 * 16 * 4096 * 4096, bytes_accessed=0, transcendentals=0),
         compiler_params=pltpu.CompilerParams(vmem_limit_bytes=8 * 2**20),
         name="conv",
@@ -241,23 +248,36 @@
     mine_r, mine = in_vmem(mine_kernel, [SMEM] + [VMEM] * 3, [narrow, wide], "mine", flops)(
         place, own_w[2], ring_w, rows
     )
-    core_r, far = in_vmem(far_kernel, [SMEM] + [VMEM] * 4, [narrow] * 2, "far", flops)(
+    half = jax.ShapeDtypeStruct((LANES, 512), jnp.bfloat16)
+    kept = jax.ShapeDtypeStruct((LANES, 512), jnp.float32)
+    core_r, far_a, far_b = in_vmem(far_kernel, [SMEM] + [VMEM] * 4, [narrow, half, half], "far", flops)(
         place, mine, core_w, diag_w, core_rows
     )
 
-    def near(n, after, kind):
-        call = in_vmem(functools.partial(near_kernel, n), [VMEM] * 6 + [ANY], [kind], "near", 2 * flops)
-        return call(own_w[n], ring_w, core_w, diag_w, mine_r, core_r, after)[0]
-
-    up = near(1, far, narrow)
-    down = near(3, up, narrow)
-    own = near(0, down, wide)
-    far = lax.ppermute(far, "chan", chan_perm(2, 0, 0))
-    up = lax.ppermute(up, "chan", chan_perm(1, 0, 0))
-    down = lax.ppermute(down, "chan", chan_perm(-1, 0, 0))
-    (two,) = in_vmem(two_kernel, [VMEM] * 2, [wide], "two", 0)(own, far)
+    def near(n, after, kinds):
+        call = in_vmem(functools.partial(near_kernel, n), [VMEM] * 6 + [ANY], kinds, "near", 2 * flops)
+        return call(own_w[n], ring_w, core_w, diag_w, mine_r, core_r, after)
+
+    up_a, up_b = near(1, far_b, [kept, half])
+    down_a, down_b = near(3, up_b, [half, kept])
+    own_a, own_b = near(0, down_a, [kept, kept])
+    upward, downward = chan_perm(1, 0, 0), chan_perm(-1, 0, 0)
+    far_a, far_b = lax.ppermute(far_a, "chan", upward), lax.ppermute(far_b, "chan", downward)
+    up_b, down_a = lax.ppermute(up_b, "chan", upward), lax.ppermute(down_a, "chan", downward)
+    (up_a,) = in_vmem(relay_kernel, [VMEM] * 2, [half], "relay", 0)(up_a, far_a)
+    (down_b,) = in_vmem(relay_kernel, [VMEM] * 2, [half], "relay", 0)(down_b, far_b)
+    up_a, down_b = lax.ppermute(up_a, "chan", upward), lax.ppermute(down_b, "chan", downward)
+    (two,) = in_vmem(two_kernel, [VMEM] * 4, [wide], "two", 0)(own_a, own_b, down_a, up_b)
     out = jax.ShapeDtypeStruct((512, 256), jnp.bfloat16)
-    return in_vmem(sum_kernel, [VMEM] * 3, [out], "sum", 0)(two, up, down)[0]
+    return pl.pallas_call(
+        sum_kernel,
+        in_specs=[VMEM] * 3,
+        out_specs=ANY,
+        out_shape=out,
+        scratch_shapes=[pltpu.VMEM((512, 256), jnp.bfloat16), pltpu.SemaphoreType.DMA((4,))],
+        compiler_params=pltpu.CompilerParams(vmem_limit_bytes=8 * 2**20),
+        name="sum",
+    )(two, up_a, down_b)
 
 
 def solution(mesh):

time: 70.2 us -> 67.8 us (0.966); the launches traced: 68.8 us -> 67.4 us
  waiting for transfers between devices: 15.3 us -> 11.2 us
  starting transfers between devices: 18.5 us -> 21.2 us
    ppermute x3 -> x6, waiting for transfers between devices: 10.6 us -> 6.57 us  [the longest x1 2.99 us: local(): lax.ppermute(down_b, 'chan', downward)]
    ppermute x3 -> x6, starting transfers between devices: 3.75 us -> 6.46 us  [the longest x1 1.76 us: local(): lax.ppermute(up_b, 'chan', upward)]
    pallas_call x6 -> x8, Pallas kernels: 2.54 us -> 2.57 us  [the longest x3 1.29 us: near(): return call(own_w[n], ring_w, core_w, diag_w, mine_r, core_r, after)]
  transfers between devices with their start and end apart: 8 -> 11, of which waited for: 5 -> 6; matrix products, arithmetic and copies ran while one was open for 0% -> 0% of each run, Pallas kernels for 17% -> 17%
where the time goes in v4:
time: 67.8 us; the launch traced here: 67.4 us
  starting transfers between devices  21.2 us (31%)
  blocking collectives  18.2 us (27%)
  Pallas kernels  14.5 us (21%)
  waiting for transfers between devices  11.2 us (17%)
  local copies, waits for them, and re-layouts  2.07 us (3%)
    all_to_all x1, blocking collectives, local(): lax.all_to_all(rows, both, 0, 0, axis_index_groups=seq_y_groups(), tiled=...  18.2 us
    all_to_all x1, starting transfers between devices, local(): recv = lax.all_to_all(send, 'seq', 0, 0, tiled=True)  11.2 us
    pallas_call x2, Pallas kernels, weight_slices(): pl.pallas_call(functools.partial(slice_kernel, parts), in_specs=[SMEM, AN...  5.08 us
    pallas_call x1, Pallas kernels, local(): pl.pallas_call(conv_kernel, out_shape=jax.ShapeDtypeStruct((N_SEQ, 2, 2,...  4.61 us
    all_to_all x1, waiting for transfers between devices, local(): recv = lax.all_to_all(send, 'seq', 0, 0, tiled=True)  4.45 us
    ppermute x1, waiting for transfers between devices, local(): lax.ppermute(down_b, 'chan', downward)  2.99 us
    ppermute x1, starting transfers between devices, local(): diag_w = lax.ppermute(diag_w, both, ring_y_perm(-1, 1))  2.79 us
    ppermute x1, waiting for transfers between devices, local(): lax.ppermute(down_a, 'chan', downward)  1.93 us
  transfers between devices with their start and end apart: 11, of which 6 were waited for; matrix products, arithmetic and copies ran while one was open for 0% of the time, Pallas kernels for 17%

profile of v4, /device:TPU:6, one launch (start us, length us, event | category | flops | bytes accessed | tf_op | source)
XLA Modules:
  0.0 67.4 jit_solution(3644828887433950111)
XLA Ops:
  0.0 1.9 %pack.1 = (bf16[16,3,2,16,128]{4,3,2,1,0:T(8,128)(2,1)}, f32[8,128]{1,0:T(8,128)}) custom-call(bf16[256,256]{1,0:T(8,128)(2,1)} %query_ref.1, bf16[256,256]{1,0:T(8,128)(2,1)} %key_ref.1, bf16[256,256]{1,0:T(8,128)(2,1)} %value_ref.1, f32[256,256]{1,0:T(8,128)} %taps_ref.1), custom_call_target="tpu_custom_call" | custom-call | tf_op jit(solution)/shard_map/pack/pallas_call | solution.py:208
  1.9 11.2 %all-to-all-start = ((bf16[16,3,2,16,128]{4,3,2,1,0:T(8,128)(2,1)}), bf16[16,3,2,16,128]{4,3,2,1,0:T(8,128)(2,1)S(1)}, u32[]{:S(2)}, u32[]{:S(2)}) async-start(bf16[16,3,2,16,128]{4,3,2,1,0:T(8,128)(2,1)} %get-tuple-element.31), calls=%async_computation | async-start | bytes 786432 | tf_op jit(solution)/shard_map/all_to_all | solution.py:231
  13.1 0.0 copy-start.5
  13.2 3.0 %weight_slices.3 = (bf16[4,256,512]{2,1,0:T(8,128)(2,1)}, bf16[4,256,512]{2,1,0:T(8,128)(2,1)}, bf16[4,256,512]{2,1,0:T(8,128)(2,1)}) custom-call(s32[1]{0:T(128)} %bitcast.place_ref, f32[8,128]{1,0:T(8,128)} %get-tuple-element.25.after_ref, bf16[256,8192]{1,0:T(8,128)(2,1)} %weight_ref.3), custom_call_target="tpu_custom_call" | custom-call | bytes 3145728 | tf_op jit(solution)/shard_map/weight_slices/pallas_call | solution.py:123
  16.2 0.8 %collective-permute-start = (bf16[4,256,512]{2,1,0:T(8,128)(2,1)}, bf16[4,256,512]{2,1,0:T(8,128)(2,1)S(1)}, u32[]{:S(2)}, u32[]{:S(2)}) collective-permute-start(bf16[4,256,512]{2,1,0:T(8,128)(2,1)} %get-tuple-element.27), channel_id=1, source_target_pairs={{0,2},{1,3},{4,6},{5,7},{8,10},{9,11},{12,14},{13,15},{16,18},{17,... | collective-permute-start | bytes 3145736 | tf_op jit(solution)/shard_map/ppermute | solution.py:223
  16.9 0.0 collective-permute-start.1
  16.9 2.8 %collective-permute-start.2 = (bf16[4,256,512]{2,1,0:T(8,128)(2,1)}, bf16[4,256,512]{2,1,0:T(8,128)(2,1)S(1)}, u32[]{:S(2)}, u32[]{:S(2)}) collective-permute-start(bf16[4,256,512]{2,1,0:T(8,128)(2,1)} %get-tuple-element.29), channel_id=1, source_target_pairs={{0,131},{1,130},{4,135},{5,134},{8,139},{9,138},{12,143},{13,142},... | collective-permute-start | bytes 3145736 | tf_op jit(solution)/shard_map/ppermute | solution.py:224
  19.7 2.1 %weight_slices.2 = (bf16[1,256,512]{2,1,0:T(8,128)(2,1)}, bf16[1,256,512]{2,1,0:T(8,128)(2,1)}, bf16[1,256,512]{2,1,0:T(8,128)(2,1)}, bf16[1,256,512]{2,1,0:T(8,128)(2,1)}) custom-call(s32[1]{0:T(128)} %bitcast.place_ref, f32[8,128]{1,0:T(8,128)} %get-tuple-element.25.after_ref, bf16[256,8192]{1,0:T(8,128)(2,1)} %weight_ref.3), custom_call_target="tpu_custom_call" | custom-call | bytes 4194304 | tf_op jit(solution)/shard_map/weight_slices/pallas_call | solution.py:123
  21.8 0.0 copy-done.5
  21.8 0.1 dynamic_slice.3
  21.9 0.1 broadcast_in_dim.2.gain_ref
  22.0 0.0 copy-start
  22.0 0.9 %copy-done = bf16[1,256,512]{2,1,0:T(8,128)(2,1)S(1)} copy-done((bf16[1,256,512]{2,1,0:T(8,128)(2,1)S(1)}, bf16[1,256,512]{2,1,0:T(8,128)(2,1)}, u32[]{:S(2)}) %copy-start) | copy-done | bytes 262168
  22.9 4.4 %all-to-all-done.recv_ref = bf16[16,3,2,16,128]{4,3,2,1,0:T(8,128)(2,1)S(1)} async-done(((bf16[16,3,2,16,128]{4,3,2,1,0:T(8,128)(2,1)}), bf16[16,3,2,16,128]{4,3,2,1,0:T(8,128)(2,1)S(1)}, u32[]{:S(2)}, u32[]{:S(2)}) %all-to-all-start) | async-done | bytes 393248 | tf_op jit(solution)/shard_map/all_to_all | solution.py:231
  27.4 0.0 copy-start.4
  27.4 4.6 %conv.1 = bf16[16,2,2,16,128]{4,3,2,1,0:T(8,128)(2,1)S(1)} custom-call(bf16[16,3,2,16,128]{4,3,2,1,0:T(8,128)(2,1)S(1)} %all-to-all-done.recv_ref, f32[16,128]{1,0:T(8,128)S(1)} %gain.1.gain_ref), custom_call_target="tpu_custom_call" | custom-call | flops 536870912 | tf_op jit(solution)/shard_map/conv/pallas_call | solution.py:232
  32.0 18.2 %all_to_all.10 = bf16[32,2,16,128]{3,2,1,0:T(8,128)(2,1)S(1)} all-to-all(bf16[32,2,16,128]{3,2,1,0:T(8,128)(2,1)S(1)} %bitcast.14), channel_id=1, replica_groups={{0,2,16,18,32,34,48,50,64,66,80,82,96,98,112,114,128,130,144,146,160,16..., dimensions={0} | all-to-all | bytes 524288 | tf_op jit(solution)/shard_map/all_to_all | solution.py:243
  50.2 0.0 collective-permute-start.3
  50.2 0.0 collective-permute-done.ring_w
  50.2 0.0 copy-start.1
  50.2 0.9 %copy-done.1 = bf16[1,256,512]{2,1,0:T(8,128)(2,1)S(1)} copy-done((bf16[1,256,512]{2,1,0:T(8,128)(2,1)S(1)}, bf16[1,256,512]{2,1,0:T(8,128)(2,1)}, u32[]{:S(2)}) %copy-start.1) | copy-done | bytes 262168
  51.2 0.0 copy-start.3
  51.2 0.4 mine.1
  51.5 0.0 collective-permute-done.1.core_w
  51.6 0.0 collective-permute-done.2.diag_w
  51.6 0.2 collective-permute-done.3.rows_ref
  51.8 0.4 far.1
  52.1 0.6 collective-permute-start.6
  52.7 1.5 %collective-permute-start.8 = (bf16[128,512]{1,0:T(8,128)(2,1)S(1)}, bf16[128,512]{1,0:T(8,128)(2,1)S(1)}, u32[]{:S(2)}, u32[]{:S(2)}) collective-permute-start(bf16[128,512]{1,0:T(8,128)(2,1)S(1)} %get-tuple-element.37.after), channel_id=1, source_target_pairs={{0,12},{1,13},{2,14},{3,15},{4,0},{5,1},{6,2},{7,3},{8,4},{9,5},{1... | collective-permute-start | bytes 393224 | tf_op jit(solution)/shard_map/ppermute | solution.py:265
  54.2 0.0 copy-done.4
  54.2 0.0 copy-start.2
  54.2 0.4 near.3
  54.7 1.8 %collective-permute-start.5 = (bf16[128,512]{1,0:T(8,128)(2,1)S(1)}, bf16[128,512]{1,0:T(8,128)(2,1)S(1)}, u32[]{:S(2)}, u32[]{:S(2)}) collective-permute-start(bf16[128,512]{1,0:T(8,128)(2,1)S(1)} %get-tuple-element.38.after), channel_id=1, source_target_pairs={{0,4},{1,5},{2,6},{3,7},{4,8},{5,9},{6,10},{7,11},{8,12},{9,13},{1... | collective-permute-start | bytes 393224 | tf_op jit(solution)/shard_map/ppermute | solution.py:266
  56.4 0.0 copy-done.3
  56.4 0.4 near.4
  56.9 0.4 collective-permute-start.4
  57.3 1.2 %collective-permute-done.6.arrived = bf16[128,512]{1,0:T(8,128)(2,1)S(1)} collective-permute-done((bf16[128,512]{1,0:T(8,128)(2,1)S(1)}, bf16[128,512]{1,0:T(8,128)(2,1)S(1)}, u32[]{:S(2)}, u32[]{:S(2)}) %collective-permute-start.6) | collective-permute-done | bytes 131104 | tf_op jit(solution)/shard_map/ppermute | solution.py:265
  58.5 1.8 %collective-permute-start.7 = (bf16[128,512]{1,0:T(8,128)(2,1)S(1)}, bf16[128,512]{1,0:T(8,128)(2,1)S(1)}, u32[]{:S(2)}, u32[]{:S(2)}) collective-permute-start(bf16[128,512]{1,0:T(8,128)(2,1)S(1)} %relay.2), channel_id=1, source_target_pairs={{0,4},{1,5},{2,6},{3,7},{4,8},{5,9},{6,10},{7,11},{8,12},{9,13},{1... | collective-permute-start | bytes 393224 | tf_op jit(solution)/shard_map/ppermute | solution.py:269
  60.3 0.0 collective-permute-done.8.arrived
  60.3 0.4 collective-permute-start.9
  60.8 0.0 copy-done.2
  60.8 0.4 near.5
  61.2 1.9 %collective-permute-done.4.above = bf16[128,512]{1,0:T(8,128)(2,1)S(1)} collective-permute-done((bf16[128,512]{1,0:T(8,128)(2,1)S(1)}, bf16[128,512]{1,0:T(8,128)(2,1)S(1)}, u32[]{:S(2)}, u32[]{:S(2)}) %collective-permute-start.4) | collective-permute-done | bytes 131104 | tf_op jit(solution)/shard_map/ppermute | solution.py:266
  63.1 0.0 collective-permute-done.5.below
  63.2 0.4 collective-permute-done.7.below
  63.6 3.0 %collective-permute-done.9.above = bf16[128,512]{1,0:T(8,128)(2,1)S(1)} collective-permute-done((bf16[128,512]{1,0:T(8,128)(2,1)S(1)}, bf16[128,512]{1,0:T(8,128)(2,1)S(1)}, u32[]{:S(2)}, u32[]{:S(2)}) %collective-permute-start.9) | collective-permute-done | bytes 131104 | tf_op jit(solution)/shard_map/ppermute | solution.py:269
  66.6 0.8 %sum.1 = bf16[512,256]{1,0:T(8,128)(2,1)} custom-call(f32[256,512]{1,0:T(8,128)S(1)} %two.1, bf16[128,512]{1,0:T(8,128)(2,1)S(1)} %collective-permute-done.7.below, bf16[128,512]{1,0:T(8,128)(2,1)S(1)} %collective-permute-done.9.above), custom_call_target="tpu_custom_call" | custom-call | tf_op jit(solution)/shard_map/sum/pallas_call | solution.py:272
  (4 shorter events, 0.1 us)
Async XLA Ops:
  1.9 25.4 %all-to-all-start = ((bf16[16,3,2,16,128]{4,3,2,1,0:T(8,128)(2,1)}), bf16[16,3,2,16,128]{4,3,2,1,0:T(8,128)(2,1)S(1)}, u32[]{:S(2)}, u32[]{:S(2)}) async-start(bf16[16,3,2,16,128]{4,3,2,1,0:T(8,128)(2,1)} %get-tuple-element.31), calls=%async_computation | async-start | bytes 786432 | tf_op jit(solution)/shard_map/all_to_all | solution.py:231
  13.1 8.7 %copy-start.5 = (f32[256]{0:T(256)S(1)}, f32[256]{0:T(256)}, u32[]{:S(2)}) copy-start(f32[256]{0:T(256)} %param.10) | copy-start | bytes 3076
  16.2 34.1 %collective-permute-start = (bf16[4,256,512]{2,1,0:T(8,128)(2,1)}, bf16[4,256,512]{2,1,0:T(8,128)(2,1)S(1)}, u32[]{:S(2)}, u32[]{:S(2)}) collective-permute-start(bf16[4,256,512]{2,1,0:T(8,128)(2,1)} %get-tuple-element.27), channel_id=1, source_target_pairs={{0,2},{1,3},{4,6},{5,7},{8,10},{9,11},{12,14},{13,15},{16,18},{17,... | collective-permute-start | bytes 3145736 | tf_op jit(solution)/shard_map/ppermute | solution.py:223
  16.9 34.6 %collective-permute-start.1 = (bf16[4,256,512]{2,1,0:T(8,128)(2,1)}, bf16[4,256,512]{2,1,0:T(8,128)(2,1)S(1)}, u32[]{:S(2)}, u32[]{:S(2)}) collective-permute-start(bf16[4,256,512]{2,1,0:T(8,128)(2,1)} %get-tuple-element.28), channel_id=1, source_target_pairs={{0,1},{1,0},{2,3},{3,2},{4,5},{5,4},{6,7},{7,6},{8,9},{9,8},{10,11... | collective-permute-start | bytes 3145736 | tf_op jit(solution)/shard_map/ppermute | solution.py:225
  16.9 34.6 %collective-permute-start.2 = (bf16[4,256,512]{2,1,0:T(8,128)(2,1)}, bf16[4,256,512]{2,1,0:T(8,128)(2,1)S(1)}, u32[]{:S(2)}, u32[]{:S(2)}) collective-permute-start(bf16[4,256,512]{2,1,0:T(8,128)(2,1)} %get-tuple-element.29), channel_id=1, source_target_pairs={{0,131},{1,130},{4,135},{5,134},{8,139},{9,138},{12,143},{13,142},... | collective-permute-start | bytes 3145736 | tf_op jit(solution)/shard_map/ppermute | solution.py:224
  22.0 1.0 %copy-start = (bf16[1,256,512]{2,1,0:T(8,128)(2,1)S(1)}, bf16[1,256,512]{2,1,0:T(8,128)(2,1)}, u32[]{:S(2)}) copy-start(bf16[1,256,512]{2,1,0:T(8,128)(2,1)} %get-tuple-element.30) | copy-start | bytes 786436
  27.4 26.9 %copy-start.4 = (bf16[1,256,512]{2,1,0:T(8,128)(2,1)S(1)}, bf16[1,256,512]{2,1,0:T(8,128)(2,1)}, u32[]{:S(2)}) copy-start(bf16[1,256,512]{2,1,0:T(8,128)(2,1)} %get-tuple-element.36) | copy-start | bytes 786436
  50.2 1.5 %collective-permute-start.3 = (bf16[16,2,2,16,128]{4,3,2,1,0:T(8,128)(2,1)S(1)}, bf16[16,2,2,16,128]{4,3,2,1,0:T(8,128)(2,1)S(1)}, u32[]{:S(2)}, u32[]{:S(2)}) collective-permute-start(bf16[16,2,2,16,128]{4,3,2,1,0:T(8,128)(2,1)S(1)} %bitcast.9), channel_id=1, source_target_pairs={{0,1},{1,0},{2,3},{3,2},{4,5},{5,4},{6,7},{7,6},{8,9},{9,8},{10,11... | collective-permute-start | bytes 786440 | tf_op jit(solution)/shard_map/ppermute | solution.py:245
  50.2 1.0 %copy-start.1 = (bf16[1,256,512]{2,1,0:T(8,128)(2,1)S(1)}, bf16[1,256,512]{2,1,0:T(8,128)(2,1)}, u32[]{:S(2)}) copy-start(bf16[1,256,512]{2,1,0:T(8,128)(2,1)} %get-tuple-element.30) | copy-start | bytes 786436
  51.2 5.3 %copy-start.3 = (bf16[1,256,512]{2,1,0:T(8,128)(2,1)S(1)}, bf16[1,256,512]{2,1,0:T(8,128)(2,1)}, u32[]{:S(2)}) copy-start(bf16[1,256,512]{2,1,0:T(8,128)(2,1)} %get-tuple-element.35) | copy-start | bytes 786436
  52.1 6.4 %collective-permute-start.6 = (bf16[128,512]{1,0:T(8,128)(2,1)S(1)}, bf16[128,512]{1,0:T(8,128)(2,1)S(1)}, u32[]{:S(2)}, u32[]{:S(2)}) collective-permute-start(bf16[128,512]{1,0:T(8,128)(2,1)S(1)} %get-tuple-element.43), channel_id=1, source_target_pairs={{0,4},{1,5},{2,6},{3,7},{4,8},{5,9},{6,10},{7,11},{8,12},{9,13},{1... | collective-permute-start | bytes 393224 | tf_op jit(solution)/shard_map/ppermute | solution.py:265
  52.7 7.6 %collective-permute-start.8 = (bf16[128,512]{1,0:T(8,128)(2,1)S(1)}, bf16[128,512]{1,0:T(8,128)(2,1)S(1)}, u32[]{:S(2)}, u32[]{:S(2)}) collective-permute-start(bf16[128,512]{1,0:T(8,128)(2,1)S(1)} %get-tuple-element.37.after), channel_id=1, source_target_pairs={{0,12},{1,13},{2,14},{3,15},{4,0},{5,1},{6,2},{7,3},{8,4},{9,5},{1... | collective-permute-start | bytes 393224 | tf_op jit(solution)/shard_map/ppermute | solution.py:265
  54.2 6.5 %copy-start.2 = (bf16[1,256,512]{2,1,0:T(8,128)(2,1)S(1)}, bf16[1,256,512]{2,1,0:T(8,128)(2,1)}, u32[]{:S(2)}) copy-start(bf16[1,256,512]{2,1,0:T(8,128)(2,1)} %get-tuple-element.26) | copy-start | bytes 786436
  54.7 8.5 %collective-permute-start.5 = (bf16[128,512]{1,0:T(8,128)(2,1)S(1)}, bf16[128,512]{1,0:T(8,128)(2,1)S(1)}, u32[]{:S(2)}, u32[]{:S(2)}) collective-permute-start(bf16[128,512]{1,0:T(8,128)(2,1)S(1)} %get-tuple-element.38.after), channel_id=1, source_target_pairs={{0,4},{1,5},{2,6},{3,7},{4,8},{5,9},{6,10},{7,11},{8,12},{9,13},{1... | collective-permute-start | bytes 393224 | tf_op jit(solution)/shard_map/ppermute | solution.py:266
  56.9 6.3 %collective-permute-start.4 = (bf16[128,512]{1,0:T(8,128)(2,1)S(1)}, bf16[128,512]{1,0:T(8,128)(2,1)S(1)}, u32[]{:S(2)}, u32[]{:S(2)}) collective-permute-start(bf16[128,512]{1,0:T(8,128)(2,1)S(1)} %get-tuple-element.39.after), channel_id=1, source_target_pairs={{0,12},{1,13},{2,14},{3,15},{4,0},{5,1},{6,2},{7,3},{8,4},{9,5},{1... | collective-permute-start | bytes 393224 | tf_op jit(solution)/shard_map/ppermute | solution.py:266
  58.5 5.0 %collective-permute-start.7 = (bf16[128,512]{1,0:T(8,128)(2,1)S(1)}, bf16[128,512]{1,0:T(8,128)(2,1)S(1)}, u32[]{:S(2)}, u32[]{:S(2)}) collective-permute-start(bf16[128,512]{1,0:T(8,128)(2,1)S(1)} %relay.2), channel_id=1, source_target_pairs={{0,4},{1,5},{2,6},{3,7},{4,8},{5,9},{6,10},{7,11},{8,12},{9,13},{1... | collective-permute-start | bytes 393224 | tf_op jit(solution)/shard_map/ppermute | solution.py:269
  60.3 6.3 %collective-permute-start.9 = (bf16[128,512]{1,0:T(8,128)(2,1)S(1)}, bf16[128,512]{1,0:T(8,128)(2,1)S(1)}, u32[]{:S(2)}, u32[]{:S(2)}) collective-permute-start(bf16[128,512]{1,0:T(8,128)(2,1)S(1)} %relay.3), channel_id=1, source_target_pairs={{0,12},{1,13},{2,14},{3,15},{4,0},{5,1},{6,2},{7,3},{8,4},{9,5},{1... | collective-permute-start | bytes 393224 | tf_op jit(solution)/shard_map/ppermute | solution.py:269

commit v5 on v4

--- a/solution.py
+++ b/solution.py
@@ -174,16 +174,30 @@
     out_ref[LANES:, :] = own_b[...] + below[...].astype(jnp.float32)
 
 
-def sum_kernel(two, below, above, out_ref, held, sems):
+def sum_kernel(part, two, relayed, *refs):
+    out_ref, held, sems = refs[-3:]
+    rows = slice(LANES * part, LANES * part + LANES)
     stores = []
-    for part in range(4):
-        at = slice(LANES * part, LANES * part + LANES)
-        held[at, :LANES] = (two[:LANES, at] + below[:, at].astype(jnp.float32)).T.astype(jnp.bfloat16)
-        held[at, LANES:] = (two[LANES:, at] + above[:, at].astype(jnp.float32)).T.astype(jnp.bfloat16)
-        stores.append(pltpu.make_async_copy(held.at[at], out_ref.at[at], sems.at[part]))
+    for piece in range(2):
+        at = slice(256 * piece, 256 * piece + 256)
+        held[at, :] = (two[rows, at] + relayed[:, at].astype(jnp.float32)).T.astype(jnp.bfloat16)
+        stores.append(pltpu.make_async_copy(held.at[at], out_ref.at[at, pl.ds(LANES * part, LANES)], sems.at[piece]))
         stores[-1].start()
     for store in stores:
         store.wait()
+
+
+def write_half(part, two, relayed, *before):
+    return pl.pallas_call(
+        functools.partial(sum_kernel, part),
+        in_specs=[VMEM] * 2 + [ANY] * len(before),
+        out_specs=ANY,
+        out_shape=jax.ShapeDtypeStruct((512, 256), jnp.bfloat16),
+        input_output_aliases={2: 0} if before else {},
+        scratch_shapes=[pltpu.VMEM((512, LANES), jnp.bfloat16), pltpu.SemaphoreType.DMA((2,))],
+        compiler_params=pltpu.CompilerParams(vmem_limit_bytes=8 * 2**20),
+        name="sum",
+    )(two, relayed, *before)
 
 
 def gain_kernel(gain_ref, after, out_ref):
@@ -268,16 +282,7 @@
     (down_b,) = in_vmem(relay_kernel, [VMEM] * 2, [half], "relay", 0)(down_b, far_b)
     up_a, down_b = lax.ppermute(up_a, "chan", upward), lax.ppermute(down_b, "chan", downward)
     (two,) = in_vmem(two_kernel, [VMEM] * 4, [wide], "two", 0)(own_a, own_b, down_a, up_b)
-    out = jax.ShapeDtypeStruct((512, 256), jnp.bfloat16)
-    return pl.pallas_call(
-        sum_kernel,
-        in_specs=[VMEM] * 3,
-        out_specs=ANY,
-        out_shape=out,
-        scratch_shapes=[pltpu.VMEM((512, 256), jnp.bfloat16), pltpu.SemaphoreType.DMA((4,))],
-        compiler_params=pltpu.CompilerParams(vmem_limit_bytes=8 * 2**20),
-        name="sum",
-    )(two, up_a, down_b)
+    return write_half(1, two, down_b, write_half(0, two, up_a))
 
 
 def solution(mesh):

time: 67.8 us -> 67.7 us (level)
  Pallas kernels: 14.5 us -> 15.3 us
  waiting for transfers between devices: 11.2 us -> 10.4 us
    ppermute x1, waiting for transfers between devices: 2.99 us -> 2.21 us  [local(): lax.ppermute(down_b, 'chan', downward)]
    pallas_call x1 -> x2, Pallas kernels: 0.83 us -> 1.55 us  [write_half(): pl.pallas_call(functools.partial(sum_kernel, part), in_specs=[VMEM] * 2 +...]
  transfers between devices with their start and end apart: 11 -> 11, of which waited for: 6 -> 6; matrix products, arithmetic and copies ran while one was open for 0% -> 0% of each run, Pallas kernels for 17% -> 18%
where the time goes in v5:
time: 67.7 us; the launch traced here: 67.4 us
  starting transfers between devices  21.2 us (31%)
  blocking collectives  18.2 us (27%)
  Pallas kernels  15.3 us (23%)
  waiting for transfers between devices  10.4 us (15%)
  local copies, waits for them, and re-layouts  2.07 us (3%)
    all_to_all x1, blocking collectives, local(): lax.all_to_all(rows, both, 0, 0, axis_index_groups=seq_y_groups(), tiled=...  18.2 us
    all_to_all x1, starting transfers between devices, local(): recv = lax.all_to_all(send, 'seq', 0, 0, tiled=True)  11.2 us
    pallas_call x2, Pallas kernels, weight_slices(): pl.pallas_call(functools.partial(slice_kernel, parts), in_specs=[SMEM, AN...  5.08 us
    pallas_call x1, Pallas kernels, local(): pl.pallas_call(conv_kernel, out_shape=jax.ShapeDtypeStruct((N_SEQ, 2, 2,...  4.61 us
    all_to_all x1, waiting for transfers between devices, local(): recv = lax.all_to_all(send, 'seq', 0, 0, tiled=True)  4.45 us
    ppermute x1, starting transfers between devices, local(): diag_w = lax.ppermute(diag_w, both, ring_y_perm(-1, 1))  2.79 us
    ppermute x1, waiting for transfers between devices, local(): lax.ppermute(down_b, 'chan', downward)  2.21 us
    ppermute x1, waiting for transfers between devices, local(): lax.ppermute(down_a, 'chan', downward)  1.93 us
  transfers between devices with their start and end apart: 11, of which 6 were waited for; matrix products, arithmetic and copies ran while one was open for 0% of the time, Pallas kernels for 18%

profile of v5, /device:TPU:6, one launch (start us, length us, event | category | flops | bytes accessed | tf_op | source)
XLA Modules:
  0.0 67.4 jit_solution(6926024441752746112)
XLA Ops:
  0.0 1.9 %pack.1 = (bf16[16,3,2,16,128]{4,3,2,1,0:T(8,128)(2,1)}, f32[8,128]{1,0:T(8,128)}) custom-call(bf16[256,256]{1,0:T(8,128)(2,1)} %query_ref.1, bf16[256,256]{1,0:T(8,128)(2,1)} %key_ref.1, bf16[256,256]{1,0:T(8,128)(2,1)} %value_ref.1, f32[256,256]{1,0:T(8,128)} %taps_ref.1), custom_call_target="tpu_custom_call" | custom-call | tf_op jit(solution)/shard_map/pack/pallas_call | solution.py:222
  1.9 11.2 %all-to-all-start = ((bf16[16,3,2,16,128]{4,3,2,1,0:T(8,128)(2,1)}), bf16[16,3,2,16,128]{4,3,2,1,0:T(8,128)(2,1)S(1)}, u32[]{:S(2)}, u32[]{:S(2)}) async-start(bf16[16,3,2,16,128]{4,3,2,1,0:T(8,128)(2,1)} %get-tuple-element.31), calls=%async_computation | async-start | bytes 786432 | tf_op jit(solution)/shard_map/all_to_all | solution.py:245
  13.1 0.0 copy-start.5
  13.2 3.0 %weight_slices.3 = (bf16[4,256,512]{2,1,0:T(8,128)(2,1)}, bf16[4,256,512]{2,1,0:T(8,128)(2,1)}, bf16[4,256,512]{2,1,0:T(8,128)(2,1)}) custom-call(s32[1]{0:T(128)} %bitcast.place_ref, f32[8,128]{1,0:T(8,128)} %get-tuple-element.25.after_ref, bf16[256,8192]{1,0:T(8,128)(2,1)} %weight_ref.3), custom_call_target="tpu_custom_call" | custom-call | bytes 3145728 | tf_op jit(solution)/shard_map/weight_slices/pallas_call | solution.py:123
  16.2 0.8 %collective-permute-start = (bf16[4,256,512]{2,1,0:T(8,128)(2,1)}, bf16[4,256,512]{2,1,0:T(8,128)(2,1)S(1)}, u32[]{:S(2)}, u32[]{:S(2)}) collective-permute-start(bf16[4,256,512]{2,1,0:T(8,128)(2,1)} %get-tuple-element.27), channel_id=1, source_target_pairs={{0,2},{1,3},{4,6},{5,7},{8,10},{9,11},{12,14},{13,15},{16,18},{17,... | collective-permute-start | bytes 3145736 | tf_op jit(solution)/shard_map/ppermute | solution.py:237
  16.9 0.0 collective-permute-start.1
  16.9 2.8 %collective-permute-start.2 = (bf16[4,256,512]{2,1,0:T(8,128)(2,1)}, bf16[4,256,512]{2,1,0:T(8,128)(2,1)S(1)}, u32[]{:S(2)}, u32[]{:S(2)}) collective-permute-start(bf16[4,256,512]{2,1,0:T(8,128)(2,1)} %get-tuple-element.29), channel_id=1, source_target_pairs={{0,131},{1,130},{4,135},{5,134},{8,139},{9,138},{12,143},{13,142},... | collective-permute-start | bytes 3145736 | tf_op jit(solution)/shard_map/ppermute | solution.py:238
  19.7 2.1 %weight_slices.2 = (bf16[1,256,512]{2,1,0:T(8,128)(2,1)}, bf16[1,256,512]{2,1,0:T(8,128)(2,1)}, bf16[1,256,512]{2,1,0:T(8,128)(2,1)}, bf16[1,256,512]{2,1,0:T(8,128)(2,1)}) custom-call(s32[1]{0:T(128)} %bitcast.place_ref, f32[8,128]{1,0:T(8,128)} %get-tuple-element.25.after_ref, bf16[256,8192]{1,0:T(8,128)(2,1)} %weight_ref.3), custom_call_target="tpu_custom_call" | custom-call | bytes 4194304 | tf_op jit(solution)/shard_map/weight_slices/pallas_call | solution.py:123
  21.8 0.0 copy-done.5
  21.8 0.1 dynamic_slice.3
  21.9 0.1 broadcast_in_dim.2.gain_ref
  22.0 0.0 copy-start
  22.0 0.9 %copy-done = bf16[1,256,512]{2,1,0:T(8,128)(2,1)S(1)} copy-done((bf16[1,256,512]{2,1,0:T(8,128)(2,1)S(1)}, bf16[1,256,512]{2,1,0:T(8,128)(2,1)}, u32[]{:S(2)}) %copy-start) | copy-done | bytes 262168
  22.9 4.4 %all-to-all-done.recv_ref = bf16[16,3,2,16,128]{4,3,2,1,0:T(8,128)(2,1)S(1)} async-done(((bf16[16,3,2,16,128]{4,3,2,1,0:T(8,128)(2,1)}), bf16[16,3,2,16,128]{4,3,2,1,0:T(8,128)(2,1)S(1)}, u32[]{:S(2)}, u32[]{:S(2)}) %all-to-all-start) | async-done | bytes 393248 | tf_op jit(solution)/shard_map/all_to_all | solution.py:245
  27.4 0.0 copy-start.4
  27.4 4.6 %conv.1 = bf16[16,2,2,16,128]{4,3,2,1,0:T(8,128)(2,1)S(1)} custom-call(bf16[16,3,2,16,128]{4,3,2,1,0:T(8,128)(2,1)S(1)} %all-to-all-done.recv_ref, f32[16,128]{1,0:T(8,128)S(1)} %gain.1.gain_ref), custom_call_target="tpu_custom_call" | custom-call | flops 536870912 | tf_op jit(solution)/shard_map/conv/pallas_call | solution.py:246
  32.0 18.2 %all_to_all.10 = bf16[32,2,16,128]{3,2,1,0:T(8,128)(2,1)S(1)} all-to-all(bf16[32,2,16,128]{3,2,1,0:T(8,128)(2,1)S(1)} %bitcast.14), channel_id=1, replica_groups={{0,2,16,18,32,34,48,50,64,66,80,82,96,98,112,114,128,130,144,146,160,16..., dimensions={0} | all-to-all | bytes 524288 | tf_op jit(solution)/shard_map/all_to_all | solution.py:257
  50.2 0.0 collective-permute-start.3
  50.2 0.0 collective-permute-done.ring_w
  50.2 0.0 copy-start.1
  50.2 0.9 %copy-done.1 = bf16[1,256,512]{2,1,0:T(8,128)(2,1)S(1)} copy-done((bf16[1,256,512]{2,1,0:T(8,128)(2,1)S(1)}, bf16[1,256,512]{2,1,0:T(8,128)(2,1)}, u32[]{:S(2)}) %copy-start.1) | copy-done | bytes 262168
  51.2 0.0 copy-start.3
  51.2 0.4 mine.1
  51.5 0.0 collective-permute-done.1.core_w
  51.6 0.0 collective-permute-done.2.diag_w
  51.6 0.2 collective-permute-done.3.rows_ref
  51.8 0.4 far.1
  52.1 0.6 collective-permute-start.8
  52.7 1.5 %collective-permute-start.6 = (bf16[128,512]{1,0:T(8,128)(2,1)S(1)}, bf16[128,512]{1,0:T(8,128)(2,1)S(1)}, u32[]{:S(2)}, u32[]{:S(2)}) collective-permute-start(bf16[128,512]{1,0:T(8,128)(2,1)S(1)} %get-tuple-element.37.after), channel_id=1, source_target_pairs={{0,12},{1,13},{2,14},{3,15},{4,0},{5,1},{6,2},{7,3},{8,4},{9,5},{1... | collective-permute-start | bytes 393224 | tf_op jit(solution)/shard_map/ppermute | solution.py:279
  54.2 0.0 copy-done.4
  54.2 0.0 copy-start.2
  54.2 0.4 near.3
  54.7 1.8 %collective-permute-start.5 = (bf16[128,512]{1,0:T(8,128)(2,1)S(1)}, bf16[128,512]{1,0:T(8,128)(2,1)S(1)}, u32[]{:S(2)}, u32[]{:S(2)}) collective-permute-start(bf16[128,512]{1,0:T(8,128)(2,1)S(1)} %get-tuple-element.38.after), channel_id=1, source_target_pairs={{0,4},{1,5},{2,6},{3,7},{4,8},{5,9},{6,10},{7,11},{8,12},{9,13},{1... | collective-permute-start | bytes 393224 | tf_op jit(solution)/shard_map/ppermute | solution.py:280
  56.4 0.0 copy-done.3
  56.4 0.4 near.4
  56.9 0.4 collective-permute-start.4
  57.3 1.2 %collective-permute-done.8.arrived = bf16[128,512]{1,0:T(8,128)(2,1)S(1)} collective-permute-done((bf16[128,512]{1,0:T(8,128)(2,1)S(1)}, bf16[128,512]{1,0:T(8,128)(2,1)S(1)}, u32[]{:S(2)}, u32[]{:S(2)}) %collective-permute-start.8) | collective-permute-done | bytes 131104 | tf_op jit(solution)/shard_map/ppermute | solution.py:279
  58.5 1.8 %collective-permute-start.9 = (bf16[128,512]{1,0:T(8,128)(2,1)S(1)}, bf16[128,512]{1,0:T(8,128)(2,1)S(1)}, u32[]{:S(2)}, u32[]{:S(2)}) collective-permute-start(bf16[128,512]{1,0:T(8,128)(2,1)S(1)} %relay.3), channel_id=1, source_target_pairs={{0,4},{1,5},{2,6},{3,7},{4,8},{5,9},{6,10},{7,11},{8,12},{9,13},{1... | collective-permute-start | bytes 393224 | tf_op jit(solution)/shard_map/ppermute | solution.py:283
  60.3 0.0 collective-permute-done.6.arrived
  60.3 0.4 collective-permute-start.7
  60.8 0.0 copy-done.2
  60.8 0.4 near.5
  61.2 1.9 %collective-permute-done.4.above = bf16[128,512]{1,0:T(8,128)(2,1)S(1)} collective-permute-done((bf16[128,512]{1,0:T(8,128)(2,1)S(1)}, bf16[128,512]{1,0:T(8,128)(2,1)S(1)}, u32[]{:S(2)}, u32[]{:S(2)}) %collective-permute-start.4) | collective-permute-done | bytes 131104 | tf_op jit(solution)/shard_map/ppermute | solution.py:280
  63.1 0.0 collective-permute-done.5.below
  63.2 0.4 collective-permute-done.9.relayed
  63.6 0.8 %sum.2.refs_0_ = bf16[512,256]{1,0:T(8,128)(2,1)} custom-call(f32[256,512]{1,0:T(8,128)S(1)} %two.1, bf16[128,512]{1,0:T(8,128)(2,1)S(1)} %collective-permute-done.9.relayed), custom_call_target="tpu_custom_call" | custom-call | tf_op jit(solution)/shard_map/sum/pallas_call | solution.py:191
  64.4 2.2 %collective-permute-done.7.relayed = bf16[128,512]{1,0:T(8,128)(2,1)S(1)} collective-permute-done((bf16[128,512]{1,0:T(8,128)(2,1)S(1)}, bf16[128,512]{1,0:T(8,128)(2,1)S(1)}, u32[]{:S(2)}, u32[]{:S(2)}) %collective-permute-start.7) | collective-permute-done | bytes 131104 | tf_op jit(solution)/shard_map/ppermute | solution.py:283
  66.6 0.8 %sum.3 = bf16[512,256]{1,0:T(8,128)(2,1)} custom-call(f32[256,512]{1,0:T(8,128)S(1)} %two.1, bf16[128,512]{1,0:T(8,128)(2,1)S(1)} %collective-permute-done.7.relayed, bf16[512,256]{1,0:T(8,128)(2,1)} %sum.2.refs_0_), custom_call_target="tpu_custom_call", output_to_operand_aliasing={{}: (2, {})} | custom-call | tf_op jit(solution)/shard_map/sum/pallas_call | solution.py:191
  (4 shorter events, 0.1 us)
Async XLA Ops:
  1.9 25.4 %all-to-all-start = ((bf16[16,3,2,16,128]{4,3,2,1,0:T(8,128)(2,1)}), bf16[16,3,2,16,128]{4,3,2,1,0:T(8,128)(2,1)S(1)}, u32[]{:S(2)}, u32[]{:S(2)}) async-start(bf16[16,3,2,16,128]{4,3,2,1,0:T(8,128)(2,1)} %get-tuple-element.31), calls=%async_computation | async-start | bytes 786432 | tf_op jit(solution)/shard_map/all_to_all | solution.py:245
  13.1 8.7 %copy-start.5 = (f32[256]{0:T(256)S(1)}, f32[256]{0:T(256)}, u32[]{:S(2)}) copy-start(f32[256]{0:T(256)} %param.10) | copy-start | bytes 3076
  16.2 34.1 %collective-permute-start = (bf16[4,256,512]{2,1,0:T(8,128)(2,1)}, bf16[4,256,512]{2,1,0:T(8,128)(2,1)S(1)}, u32[]{:S(2)}, u32[]{:S(2)}) collective-permute-start(bf16[4,256,512]{2,1,0:T(8,128)(2,1)} %get-tuple-element.27), channel_id=1, source_target_pairs={{0,2},{1,3},{4,6},{5,7},{8,10},{9,11},{12,14},{13,15},{16,18},{17,... | collective-permute-start | bytes 3145736 | tf_op jit(solution)/shard_map/ppermute | solution.py:237
  16.9 34.6 %collective-permute-start.1 = (bf16[4,256,512]{2,1,0:T(8,128)(2,1)}, bf16[4,256,512]{2,1,0:T(8,128)(2,1)S(1)}, u32[]{:S(2)}, u32[]{:S(2)}) collective-permute-start(bf16[4,256,512]{2,1,0:T(8,128)(2,1)} %get-tuple-element.28), channel_id=1, source_target_pairs={{0,1},{1,0},{2,3},{3,2},{4,5},{5,4},{6,7},{7,6},{8,9},{9,8},{10,11... | collective-permute-start | bytes 3145736 | tf_op jit(solution)/shard_map/ppermute | solution.py:239
  16.9 34.6 %collective-permute-start.2 = (bf16[4,256,512]{2,1,0:T(8,128)(2,1)}, bf16[4,256,512]{2,1,0:T(8,128)(2,1)S(1)}, u32[]{:S(2)}, u32[]{:S(2)}) collective-permute-start(bf16[4,256,512]{2,1,0:T(8,128)(2,1)} %get-tuple-element.29), channel_id=1, source_target_pairs={{0,131},{1,130},{4,135},{5,134},{8,139},{9,138},{12,143},{13,142},... | collective-permute-start | bytes 3145736 | tf_op jit(solution)/shard_map/ppermute | solution.py:238
  22.0 1.0 %copy-start = (bf16[1,256,512]{2,1,0:T(8,128)(2,1)S(1)}, bf16[1,256,512]{2,1,0:T(8,128)(2,1)}, u32[]{:S(2)}) copy-start(bf16[1,256,512]{2,1,0:T(8,128)(2,1)} %get-tuple-element.30) | copy-start | bytes 786436
  27.4 26.9 %copy-start.4 = (bf16[1,256,512]{2,1,0:T(8,128)(2,1)S(1)}, bf16[1,256,512]{2,1,0:T(8,128)(2,1)}, u32[]{:S(2)}) copy-start(bf16[1,256,512]{2,1,0:T(8,128)(2,1)} %get-tuple-element.36) | copy-start | bytes 786436
  50.2 1.5 %collective-permute-start.3 = (bf16[16,2,2,16,128]{4,3,2,1,0:T(8,128)(2,1)S(1)}, bf16[16,2,2,16,128]{4,3,2,1,0:T(8,128)(2,1)S(1)}, u32[]{:S(2)}, u32[]{:S(2)}) collective-permute-start(bf16[16,2,2,16,128]{4,3,2,1,0:T(8,128)(2,1)S(1)} %bitcast.9), channel_id=1, source_target_pairs={{0,1},{1,0},{2,3},{3,2},{4,5},{5,4},{6,7},{7,6},{8,9},{9,8},{10,11... | collective-permute-start | bytes 786440 | tf_op jit(solution)/shard_map/ppermute | solution.py:259
  50.2 1.0 %copy-start.1 = (bf16[1,256,512]{2,1,0:T(8,128)(2,1)S(1)}, bf16[1,256,512]{2,1,0:T(8,128)(2,1)}, u32[]{:S(2)}) copy-start(bf16[1,256,512]{2,1,0:T(8,128)(2,1)} %get-tuple-element.30) | copy-start | bytes 786436
  51.2 5.3 %copy-start.3 = (bf16[1,256,512]{2,1,0:T(8,128)(2,1)S(1)}, bf16[1,256,512]{2,1,0:T(8,128)(2,1)}, u32[]{:S(2)}) copy-start(bf16[1,256,512]{2,1,0:T(8,128)(2,1)} %get-tuple-element.35) | copy-start | bytes 786436
  52.1 6.4 %collective-permute-start.8 = (bf16[128,512]{1,0:T(8,128)(2,1)S(1)}, bf16[128,512]{1,0:T(8,128)(2,1)S(1)}, u32[]{:S(2)}, u32[]{:S(2)}) collective-permute-start(bf16[128,512]{1,0:T(8,128)(2,1)S(1)} %get-tuple-element.44), channel_id=1, source_target_pairs={{0,4},{1,5},{2,6},{3,7},{4,8},{5,9},{6,10},{7,11},{8,12},{9,13},{1... | collective-permute-start | bytes 393224 | tf_op jit(solution)/shard_map/ppermute | solution.py:279
  52.7 7.6 %collective-permute-start.6 = (bf16[128,512]{1,0:T(8,128)(2,1)S(1)}, bf16[128,512]{1,0:T(8,128)(2,1)S(1)}, u32[]{:S(2)}, u32[]{:S(2)}) collective-permute-start(bf16[128,512]{1,0:T(8,128)(2,1)S(1)} %get-tuple-element.37.after), channel_id=1, source_target_pairs={{0,12},{1,13},{2,14},{3,15},{4,0},{5,1},{6,2},{7,3},{8,4},{9,5},{1... | collective-permute-start | bytes 393224 | tf_op jit(solution)/shard_map/ppermute | solution.py:279
  54.2 6.5 %copy-start.2 = (bf16[1,256,512]{2,1,0:T(8,128)(2,1)S(1)}, bf16[1,256,512]{2,1,0:T(8,128)(2,1)}, u32[]{:S(2)}) copy-start(bf16[1,256,512]{2,1,0:T(8,128)(2,1)} %get-tuple-element.26) | copy-start | bytes 786436
  54.7 8.5 %collective-permute-start.5 = (bf16[128,512]{1,0:T(8,128)(2,1)S(1)}, bf16[128,512]{1,0:T(8,128)(2,1)S(1)}, u32[]{:S(2)}, u32[]{:S(2)}) collective-permute-start(bf16[128,512]{1,0:T(8,128)(2,1)S(1)} %get-tuple-element.38.after), channel_id=1, source_target_pairs={{0,4},{1,5},{2,6},{3,7},{4,8},{5,9},{6,10},{7,11},{8,12},{9,13},{1... | collective-permute-start | bytes 393224 | tf_op jit(solution)/shard_map/ppermute | solution.py:280
  56.9 6.3 %collective-permute-start.4 = (bf16[128,512]{1,0:T(8,128)(2,1)S(1)}, bf16[128,512]{1,0:T(8,128)(2,1)S(1)}, u32[]{:S(2)}, u32[]{:S(2)}) collective-permute-start(bf16[128,512]{1,0:T(8,128)(2,1)S(1)} %get-tuple-element.39.after), channel_id=1, source_target_pairs={{0,12},{1,13},{2,14},{3,15},{4,0},{5,1},{6,2},{7,3},{8,4},{9,5},{1... | collective-permute-start | bytes 393224 | tf_op jit(solution)/shard_map/ppermute | solution.py:280
  58.5 5.0 %collective-permute-start.9 = (bf16[128,512]{1,0:T(8,128)(2,1)S(1)}, bf16[128,512]{1,0:T(8,128)(2,1)S(1)}, u32[]{:S(2)}, u32[]{:S(2)}) collective-permute-start(bf16[128,512]{1,0:T(8,128)(2,1)S(1)} %relay.3), channel_id=1, source_target_pairs={{0,4},{1,5},{2,6},{3,7},{4,8},{5,9},{6,10},{7,11},{8,12},{9,13},{1... | collective-permute-start | bytes 393224 | tf_op jit(solution)/shard_map/ppermute | solution.py:283
  60.3 6.3 %collective-permute-start.7 = (bf16[128,512]{1,0:T(8,128)(2,1)S(1)}, bf16[128,512]{1,0:T(8,128)(2,1)S(1)}, u32[]{:S(2)}, u32[]{:S(2)}) collective-permute-start(bf16[128,512]{1,0:T(8,128)(2,1)S(1)} %relay.2), channel_id=1, source_target_pairs={{0,12},{1,13},{2,14},{3,15},{4,0},{5,1},{6,2},{7,3},{8,4},{9,5},{1... | collective-permute-start | bytes 393224 | tf_op jit(solution)/shard_map/ppermute | solution.py:283
